TPU v7x, 128 devices: a whole 4x4x4 slice. The times are simulated.
128 devices in a mesh: jpair: 8 (over z, y_lo), row: 16 (over x, y_hi, core).
Axes of the slice: x: 4, y: 4 (y_hi: 2, y_lo: 2; y = y_hi * 2 + y_lo), z: 4, core: 2. Of those that a mesh axis runs over, the one named last changes fastest.
Arguments:
- s_real: bfloat16 [8, 3072, 3072], P('jpair', 'row'), may hold values from -0.67578125 to 0.67578125
- s_imag: bfloat16 [8, 3072, 3072], P('jpair', 'row'), may hold values from -0.67578125 to 0.67578125
- chan_l: int32 [8, 3072], P('jpair'), may hold values from 0 to 31
- counts: int32 [8], P('jpair'), may hold values from 2304 to 2688, as said below
- jlevel: int32 [8], P('jpair'), may hold values from 0 to 47
- allowed: int32 [32, 32], replicated, may hold values 0 or 1
- recoup: float32 [32, 32], replicated, may hold values from 0.3 to 3
Outputs:
- relax: float32 [8, 3072, 3072], P('jpair', 'row')
Inputs may be any that keep to these rules, and one draw needn't show every extreme that they name: `counts`: every block has at least three quarters of its channels open and at most 2688; some block has exactly 2688 open.
All inputs are finite; a program needn't handle non-finite values.
Results may differ from a plain program's by a relative error of at most 0.0003.
Values may be sent and summed in bfloat16 or wider, within the bound.
A program may use at most 128 MiB of HBM per device.

v0:
```python
import jax
import jax.numpy as jnp
from jax import lax
from jax.sharding import PartitionSpec as P


def partner(value, axis, stride):
    mask = 2**stride
    pairs = [(source, source ^ mask) for source in range(lax.axis_size(axis))]
    return lax.ppermute(value, axis, pairs)


def one_hot_rows(labels, levels):
    return (labels[:, None] == jnp.arange(levels)[None, :]).astype(jnp.float32)


def per_device(s_real, s_imag, chan_l, counts, jlevel, allowed, recoup):
    rows_here = s_real.shape[1]
    full_width = s_real.shape[2]
    levels = allowed.shape[0]
    row_rank = lax.axis_index("row")
    parity = lax.axis_index("jpair") % 2
    is_upper = parity == 0
    row_ids = row_rank * rows_here + jnp.arange(rows_here)
    col_ids = jnp.arange(full_width)
    open_count = counts[0]
    both_live = (row_ids < open_count)[:, None] & (col_ids < open_count)[None, :]
    zeros_bf = jnp.zeros((rows_here, full_width), jnp.bfloat16)
    mine_re = jnp.where(both_live, s_real[0], zeros_bf)
    mine_im = jnp.where(both_live, s_imag[0], zeros_bf)
    other_re, other_im, other_l, other_count, other_level = partner(
        (mine_re, mine_im, chan_l, counts, jlevel), "jpair", 0
    )
    up_re = jnp.where(is_upper, mine_re, other_re)
    up_im = jnp.where(is_upper, mine_im, other_im)
    low_re = jnp.where(is_upper, other_re, mine_re)
    low_im = jnp.where(is_upper, other_im, mine_im)
    upper_l = jnp.where(is_upper, chan_l[0], other_l[0])
    lower_l = jnp.where(is_upper, other_l[0], chan_l[0])
    upper_j = jnp.where(is_upper, jlevel[0], other_level[0])
    lower_j = jnp.where(is_upper, other_level[0], jlevel[0])
    left_side = jnp.concatenate([up_re, up_im], 0)
    right_side = jnp.where(
        is_upper, jnp.concatenate([low_re, low_im], 0), jnp.concatenate([low_im, -low_re], 0)
    )
    summed = lax.psum_scatter(
        lax.dot_general(
            left_side, right_side, (((0,), (0,)), ((), ())), preferred_element_type=jnp.float32
        ),
        "row",
        scatter_dimension=0,
        tiled=True,
    )
    weight_table = recoup * allowed.astype(jnp.float32)
    slab_labels = lax.dynamic_slice_in_dim(upper_l, row_rank * rows_here, rows_here, 0)
    rows_hot = one_hot_rows(slab_labels, levels)
    cols_hot = one_hot_rows(lower_l, levels)
    picked = jnp.dot(rows_hot, weight_table, precision=lax.Precision.HIGHEST)
    weight = jnp.dot(picked, cols_hot.T, precision=lax.Precision.HIGHEST)
    upper_deg = (2 * upper_j + 1).astype(jnp.float32)
    lower_deg = (2 * lower_j + 1).astype(jnp.float32)
    factor = 2.0 * lower_deg / (upper_deg + lower_deg)
    return (factor * weight * summed)[None]


def solution(mesh):
    placed = (
        P("jpair", "row", None),
        P("jpair", "row", None),
        P("jpair", None),
        P("jpair"),
        P("jpair"),
        P(),
        P(),
    )
    return jax.shard_map(
        per_device, mesh=mesh, in_specs=placed, out_specs=P("jpair", "row", None), check_vma=False
    )
```

profile of v0, /device:TPU:1, one launch (start us, length us, event | category | flops | bytes accessed | tf_op | source)
XLA Modules:
  0.0 362.8 jit_solution(6924274270449019727)
XLA Ops:
  6.5 0.0 reduce-scatter.2.cloned.1.call-start
  7.2 2.3 and_select_fusion.1
  9.5 2.2 collective-permute-start.2
  11.7 0.1 collective-permute-start.3
  11.8 25.2 %collective-permute-done.2 = bf16[192,3072]{1,0:T(8,128)(2,1)S(1)} collective-permute-done((bf16[192,3072]{1,0:T(8,128)(2,1)S(1)}, bf16[192,3072]{1,0:T(8,128)(2,1)S(1)}, u32[]{:S(2)}, u32[]{:S(2)}) %collective-permute-start.2) | collective-permute-done | bytes 1179680 | tf_op jit(solution)/shard_map/ppermute | solution.py:10
  37.0 1.7 fusion.18
  38.7 23.7 %collective-permute-done.3 = bf16[192,3072]{1,0:T(8,128)(2,1)} collective-permute-done((bf16[192,3072]{1,0:T(8,128)(2,1)S(1)}, bf16[192,3072]{1,0:T(8,128)(2,1)}, u32[]{:S(2)}, u32[]{:S(2)}) %collective-permute-start.3) | collective-permute-done | bytes 1179680 | tf_op jit(solution)/shard_map/ppermute | solution.py:10
  62.4 1.4 broadcast_select_fusion
  63.8 18.8 %fusion.2 = f32[3072,3072]{1,0:T(8,128)} fusion(bf16[192,3072]{1,0:T(8,128)(2,1)S(1)} %get-tuple-element.9, bf16[192,3072]{1,0:T(8,128)(2,1)} %get-tuple-element.7, bf16[192,3072]{1,0:T(8,128)(2,1)S(1)} %get-tuple-element.8, bf16[192,3072]{1,0:T(8,128)(2,1)} %get-tuple-element.6, bf16[192,3072]{1,0:T(8,128)(2,1)S(1)} %get-tuple-element.5, pred[]{:T(512)S(6)} %eq.16), kind=kOutput, calls=%fused_computation.5 | convolution fusion | flops 7263092736 | bytes 43646976 | tf_op jit(solution)/shard_map/dot_general | solution.py:47
  82.6 0.0 copy-start.2
  82.6 0.0 copy-start
  82.6 0.0 copy-start.1
  82.6 0.0 reduce-scatter.2.cloned.1.call-update
  82.6 0.7 copy-done.2
  83.3 1.5 collective-permute-start.1
  84.9 0.0 collective-permute-start
  85.6 1.9 collective-permute-done
  88.8 0.0 collective-permute-done.1
  88.8 0.1 broadcast_select_fusion.5
  88.9 0.0 copy-done
  88.9 0.0 copy-done.1
  88.9 0.2 fusion.13
  89.2 262.5 %reduce-scatter.2.cloned.1.call-done = f32[192,3072]{1,0:T(8,128)} async-done(((f32[3072,3072]{1,0:T(8,128)}), f32[192,3072]{1,0:T(8,128)}) %reduce-scatter.2.cloned.1.call-update) | async-done | bytes 2359312 | tf_op jit(solution)/shard_map/reduce_scatter | solution.py:46
  351.7 4.2 %fusion.1 = f32[1,192,3072]{2,1,0:T(8,128)} fusion(f32[192,3072]{1,0:T(8,128)} %reduce-scatter.2.cloned.1.call-done, f32[192,32]{1,0:T(8,128)S(1)} %fusion.13, f32[]{:T(128)S(6)} %div.3, s32[3072]{0:T(1024)S(1)} %bitcast.16), kind=kOutput, calls=%fused_computation.2 | convolution fusion | flops 227770368 | bytes 4755460 | tf_op jit(solution)/shard_map/dot_general | solution.py:59
  (3 shorter events, 0.0 us)
Async XLA Ops:
  6.5 345.2 %reduce-scatter.2.cloned.1.call-start = ((), (), s32[]{:S(2)}) async-start(), calls=%async_computation.1 | async-start | bytes 40108032 | tf_op jit(solution)/shard_map/reduce_scatter | solution.py:46
  9.5 27.5 %collective-permute-start.2 = (bf16[192,3072]{1,0:T(8,128)(2,1)S(1)}, bf16[192,3072]{1,0:T(8,128)(2,1)S(1)}, u32[]{:S(2)}, u32[]{:S(2)}) collective-permute-start(bf16[192,3072]{1,0:T(8,128)(2,1)S(1)} %get-tuple-element.10), channel_id=1, source_target_pairs={{0,16},{16,0},{32,48},{48,32},{64,80},{80,64},{96,112},{112,96},{1... | collective-permute-start | bytes 3538952 | tf_op jit(solution)/shard_map/ppermute | solution.py:10
  11.7 50.7 %collective-permute-start.3 = (bf16[192,3072]{1,0:T(8,128)(2,1)S(1)}, bf16[192,3072]{1,0:T(8,128)(2,1)}, u32[]{:S(2)}, u32[]{:S(2)}) collective-permute-start(bf16[192,3072]{1,0:T(8,128)(2,1)S(1)} %get-tuple-element.11), channel_id=1, source_target_pairs={{0,16},{16,0},{32,48},{48,32},{64,80},{80,64},{96,112},{112,96},{1... | collective-permute-start | bytes 3538952 | tf_op jit(solution)/shard_map/ppermute | solution.py:10
  82.6 0.7 copy-start.2
  82.6 6.3 %copy-start = (f32[32,32]{1,0:T(8,128)S(1)}, f32[32,32]{1,0:T(8,128)}, u32[]{:S(2)}) copy-start(f32[32,32]{1,0:T(8,128)} %param.13) | copy-start | bytes 12292
  82.6 6.3 %copy-start.1 = (s32[32,32]{1,0:T(8,128)S(1)}, s32[32,32]{1,0:T(8,128)}, u32[]{:S(2)}) copy-start(s32[32,32]{1,0:T(8,128)} %param.12) | copy-start | bytes 12292
  83.3 5.5 %collective-permute-start.1 = (s32[1,3072]{1,0:T(1,128)S(1)}, s32[1,3072]{1,0:T(1,128)S(1)}, u32[]{:S(2)}, u32[]{:S(2)}) collective-permute-start(s32[1,3072]{1,0:T(1,128)S(1)} %copy-done.2), channel_id=1, source_target_pairs={{0,16},{16,0},{32,48},{48,32},{64,80},{80,64},{96,112},{112,96},{1... | collective-permute-start | bytes 36872 | tf_op jit(solution)/shard_map/ppermute | solution.py:10
  84.9 2.6 collective-permute-start
Sparse Core Ops, SparseCore 0:
  82.7 268.9 reduce-scatter.1
where the time goes:
time: 364 us; the launch traced here: 363 us
  waiting for transfers between devices  313 us (86%)
  matrix products  23.2 us (6%)
  between operations  16.1 us (4%)
  other arithmetic  5.49 us (2%)
  starting transfers between devices  3.88 us (1%)
    reduce_scatter x1, waiting for transfers between devices, per_device(): lax.psum_scatter(lax.dot_general(left_side, right_side, (((0,), (0,)), ((...  263 us
    ppermute x4, waiting for transfers between devices, partner(): return lax.ppermute(value, axis, pairs)  50.8 us
    dot_general x1, matrix products, per_device(): lax.dot_general(left_side, right_side, (((0,), (0,)), ((), ())), preferre...  18.8 us
  transfers between devices with their start and end apart: 5, of which 4 were waited for; matrix products, arithmetic and copies ran while one was open for 1% of the time, Pallas kernels for 0%

commit v1 on v0

v1 whole, which is shorter than its diff:
```python
import functools

import jax
import jax.numpy as jnp
from jax import lax
from jax.experimental import pallas as pl
from jax.experimental.pallas import tpu as pltpu
from jax.sharding import PartitionSpec as P

MESH = pl.DeviceIdType.MESH
LANES = 128


def plan(rows, width):
    live = 14 * rows
    upper = 4 * rows
    main = live // LANES // 4 * LANES
    extra = live - 4 * main
    return live, upper, main, extra, main + extra


def kernel(
    rows, width, re_ref, im_ref, meta_ref, table_ref, out_ref,
    up, low, swapped, acc, other, ready, weight, zeros, meta,
    send_up, recv_up, send_low, recv_low, send_sum, recv_sum, send_out, recv_out, local_sem,
):
    live, upper, main, extra, lower = plan(rows, width)
    j, r = lax.axis_index("jpair"), lax.axis_index("row")
    pair, parity = j // 2, j % 2
    x, half, core = r // 4, (r // 2) % 2, r % 2
    y = 2 * half + parity
    is_upper, is_lower = parity == 0, parity == 1
    source = (re_ref, im_ref)

    def device(dx, dy, dcore=0):
        to_x, to_y = (x + dx) % 4, (y + dy) % 4
        return (2 * pair + to_y % 2, 4 * to_x + 2 * (to_y // 2) + (core + dcore) % 2)

    def remote(src, dst, send, recv, where):
        return pltpu.make_async_remote_copy(
            src_ref=src, dst_ref=dst, send_sem=send, recv_sem=recv, device_id=where, device_id_type=MESH
        )

    barrier = pltpu.get_barrier_semaphore()
    greeted = [(1, 0, 0), (3, 0, 0), (2, 0, 0), (0, 1, 0), (0, 3, 0), (0, 2, 0), (0, 0, 1)]
    for offset in greeted:
        pl.semaphore_signal(barrier, inc=1, device_id=device(*offset), device_id_type=MESH)
    pl.semaphore_wait(barrier, len(greeted))

    def slab_at(dx, dhalf):
        return 2 * ((x + dx) % 4) + (half + dhalf) % 2

    def piece(buffer, slab, part):
        return buffer.at[pl.ds(pl.multiple_of(slab * (2 * rows) + part * rows, rows), rows)]

    pending = []

    def send(when, copy):
        pl.when(when)(copy.start)
        pending.append((when, copy))

    def arrived(when, buffer, sems, slab, part):
        @pl.when(when)
        def _():
            here = piece(buffer, slab, part)
            remote(here, here, send_up.at[0], sems.at[slab, part], device(1, 0)).wait_recv()

    my_slab = slab_at(0, 0)
    have_rows = my_slab < 7
    up_from = is_upper & have_rows
    low_from = is_lower & have_rows

    partner = device(0, 1 - 2 * parity)
    meta_copy = remote(meta_ref, meta.at[pl.ds(0, 1)], local_sem.at[0], local_sem.at[1], partner)
    meta_copy.start()

    def up_columns(part, to_x):
        return source[part].at[0, :, pl.ds(pl.multiple_of(to_x * upper, LANES), upper)]

    def low_columns(part, to_y):
        return source[part].at[0, :, pl.ds(pl.multiple_of(to_y * main, LANES), lower)]

    for part in range(2):
        for n, dy in enumerate((1, 3)):
            send(up_from, remote(
                up_columns(part, x), piece(up, my_slab, part),
                send_up.at[6 + 2 * n + part], recv_up.at[my_slab, part], device(0, dy)))
    for n, dx in enumerate((1, 3, 2)):
        for part in range(2):
            send(up_from, remote(
                up_columns(part, (x + dx) % 4), piece(up, my_slab, part),
                send_up.at[2 * n + part], recv_up.at[my_slab, part], device(dx, 0)))
    for n, dy in enumerate((1, 3, 2)):
        for part in range(2):
            send(low_from, remote(
                low_columns(part, (y + dy) % 4), piece(low, my_slab, part),
                send_low.at[2 * n + part], recv_low.at[my_slab, part], device(0, dy)))
    for part in range(2):
        for n, dx in enumerate((1, 3)):
            send(low_from, remote(
                low_columns(part, y), piece(low, my_slab, part),
                send_low.at[6 + 2 * n + part], recv_low.at[my_slab, part], device(dx, 0)))

    own = []
    for part in range(2):
        own.append((up_from, pltpu.make_async_copy(
            up_columns(part, x), piece(up, my_slab, part), local_sem.at[2 + part])))
        own.append((low_from, pltpu.make_async_copy(
            low_columns(part, y), piece(low, my_slab, part), local_sem.at[2 + part])))
    for when, copy in own:
        pl.when(when)(copy.start)

    zeros[...] = jnp.zeros_like(zeros)
    fills = [(pl.program_id(0) == 0, width - 2 * rows)]
    fills += [(my_slab == 7, n * 2 * rows) for n in range(7)]
    blank = []
    for n, (when, start) in enumerate(fills):
        blank.append((when, pltpu.make_async_copy(
            zeros, out_ref.at[0, :, pl.ds(start, 2 * rows)], local_sem.at[4 + n])))
    for when, copy in blank:
        pl.when(when)(copy.start)
    acc[...] = jnp.zeros_like(acc)

    meta_copy.wait()
    mine, theirs = meta_ref[...], meta[0:1, :]
    first = jnp.where(is_upper, mine, theirs)
    second = jnp.where(is_upper, theirs, mine)
    upper_count, lower_count = first[:, width:width + 1], second[:, width:width + 1]
    upper_deg = (2 * first[:, width + LANES:width + LANES + 1] + 1).astype(jnp.float32)
    lower_deg = (2 * second[:, width + LANES:width + LANES + 1] + 1).astype(jnp.float32)
    factor = 2.0 * lower_deg / (upper_deg + lower_deg)
    meta[1:2, :] = first
    meta[2:3, :] = second
    levels = table_ref.shape[0]
    c_start = pl.multiple_of(x * upper, LANES)
    d_start = pl.multiple_of(y * main, LANES)
    c_labels = meta[1:2, pl.ds(c_start, upper)]
    d_labels = meta[2:3, pl.ds(d_start, lower)]
    c_open = c_start + lax.broadcasted_iota(jnp.int32, (1, upper), 1) < upper_count
    d_open = d_start + lax.broadcasted_iota(jnp.int32, (1, lower), 1) < lower_count
    c_labels = jnp.where(c_open, c_labels, -1)
    d_labels = jnp.where(d_open, d_labels, -1)
    c_hot = (lax.broadcasted_iota(jnp.int32, (levels, upper), 0) == c_labels).astype(jnp.float32)
    d_hot = (lax.broadcasted_iota(jnp.int32, (levels, lower), 0) == d_labels).astype(jnp.float32)
    picked = factor * jnp.dot(
        table_ref[...], d_hot, precision=lax.Precision.HIGHEST, preferred_element_type=jnp.float32)
    weight[...] = lax.dot_general(
        c_hot, picked, (((0,), (0,)), ((), ())),
        precision=lax.Precision.HIGHEST, preferred_element_type=jnp.float32)
    least = jnp.minimum(upper_count, lower_count)
    for when, copy in own:
        pl.when(when)(copy.wait)

    tile = min(256, upper)

    def accumulate(slab):
        @pl.when(slab < 7)
        def _():
            row = pl.multiple_of(slab * 2 * rows, rows)
            first_row = (slab // 2) * (4 * rows) + (slab % 2) * (2 * rows) + core * rows
            row_ids = first_row + lax.broadcasted_iota(jnp.int32, (rows, lower), 0)
            keep = (row_ids < least).astype(jnp.float32).astype(jnp.bfloat16)
            low_re = low[pl.ds(row, rows)] * keep
            low_im = low[pl.ds(pl.multiple_of(row + rows, rows), rows)] * keep
            swapped[0, :rows] = low_re
            swapped[0, rows:] = low_im
            swapped[1, :rows] = low_im
            swapped[1, rows:] = -low_re

            @pl.loop(0, upper // tile)
            def _(n):
                start = pl.multiple_of(n * tile, tile)
                left = up[pl.ds(row, 2 * rows), pl.ds(start, tile)]
                for part in range(2):
                    acc[part, pl.ds(start, tile)] += lax.dot_general(
                        left, swapped[part], (((0,), (0,)), ((), ())), preferred_element_type=jnp.float32)

    used = {"up": 10, "low": 10}

    def on_up(when, slab, part, dy):
        n = used["up"]
        used["up"] += 1
        here = piece(up, slab, part)
        send(when, remote(here, here, send_up.at[n], recv_up.at[slab, part], device(0, dy)))

    def on_low(when, slab, part, dx):
        n = used["low"]
        used["low"] += 1
        here = piece(low, slab, part)
        send(when, remote(here, here, send_low.at[n], recv_low.at[slab, part], device(dx, 0)))

    def own_low(dhalf):
        slab = slab_at(0, dhalf)
        when = (is_upper if dhalf == 0 else (slab >= 0)) & (slab < 7)
        for part in range(2):
            arrived(when, low, recv_low, slab, part)
            for dx in (1, 3):
                on_low(when, slab, part, dx)

    def next_low(dx, dhalf):
        slab = slab_at(dx, dhalf)
        when = slab < 7
        first_part = 0 if dx == 3 else 1
        for part in (first_part, 1 - first_part):
            arrived(when, low, recv_low, slab, part)
            if part == first_part:
                on_low(when, slab, part, 4 - dx)

    def far_low(dhalf):
        slab = slab_at(2, dhalf)
        for part in range(2):
            arrived(slab < 7, low, recv_low, slab, part)

    def even_up(dx):
        slab = slab_at(dx, 0)
        when = is_upper & (slab < 7)
        for part in range(2):
            arrived(when, up, recv_up, slab, part)
            for dy in (1, 3):
                on_up(when, slab, part, dy)

    def odd_up(dx):
        for dy, dhalf in ((3, 0), (1, 1)):
            slab = slab_at(dx, dhalf)
            when = is_lower & (slab < 7)
            first_part = 0 if dy == 3 else 1
            for part in (first_part, 1 - first_part):
                arrived(when, up, recv_up, slab, part)
                if part == first_part:
                    on_up(when, slab, part, 4 - dy)

    def far_up(dx):
        slab = slab_at(dx, 1)
        for part in range(2):
            arrived(is_upper & (slab < 7), up, recv_up, slab, part)

    odd_up(0)
    own_low(0)
    own_low(1)
    accumulate(slab_at(0, 0))
    even_up(1)
    even_up(3)
    next_low(1, 0)
    next_low(3, 0)
    next_low(1, 1)
    next_low(3, 1)
    odd_up(1)
    odd_up(3)
    even_up(2)
    far_up(0)
    accumulate(slab_at(0, 1))
    accumulate(slab_at(1, 0))
    accumulate(slab_at(3, 0))
    odd_up(2)
    far_up(1)
    accumulate(slab_at(1, 1))
    far_up(3)
    accumulate(slab_at(3, 1))
    far_low(0)
    accumulate(slab_at(2, 0))
    far_low(1)
    far_up(2)
    accumulate(slab_at(2, 1))

    order = (2, 1, 3, 0)

    def rows_of(to_y, of_core):
        return pl.ds(pl.multiple_of((to_y // 2) * (2 * rows) + of_core * rows, rows), rows)

    sums = []
    for n, dy in enumerate(order):
        to_y = (y + dy) % 4
        when = (x < 3) | (to_y < 2)
        copy = remote(
            acc.at[to_y % 2, rows_of(to_y, 1 - core)], other.at[n], send_sum.at[n], recv_sum.at[n], device(0, 0, 1))
        pl.when(when)(copy.start)
        sums.append((when, copy))

    def out_copy(n, dy, start, count, sems, last):
        dst = out_ref.at[0, :, pl.ds(start, count)]
        src = ready.at[n, :, pl.ds(last, count)]
        return src, dst

    finish = []
    for n, dy in enumerate(order):
        to_y = (y + dy) % 4
        when, copy = sums[n]
        main_src = ready.at[n, :, pl.ds(0, main)]
        main_dst = out_ref.at[0, :, pl.ds(d_start, main)]
        extra_src = ready.at[n, :, pl.ds(main, extra)]
        extra_dst = out_ref.at[0, :, pl.ds(4 * main, extra)]
        if dy == 0:
            copies = [
                (when, pltpu.make_async_copy(main_src, main_dst, local_sem.at[12])),
                (when & (y == 3), pltpu.make_async_copy(extra_src, extra_dst, local_sem.at[13])),
            ]
        else:
            copies = [
                (when, remote(main_src, main_dst, send_out.at[0, n], recv_out.at[0, y], device(0, dy))),
                (when & (y == 3), remote(extra_src, extra_dst, send_out.at[1, n], recv_out.at[1, y], device(0, dy))),
            ]

        @pl.when(when)
        def _(n=n, to_y=to_y, copy=copy):
            copy.wait_recv()
            keep = rows_of(to_y, core)
            ready[n] = weight[keep] * (acc[to_y % 2, keep] + other[n])

        for start_when, out in copies:
            pl.when(start_when)(out.start)
        finish.append((dy, copies))

    for when, copy in pending:
        pl.when(when)(copy.wait_send)
    for when, copy in sums:
        pl.when(when)(copy.wait_send)
    for when, copy in blank:
        pl.when(when)(copy.wait)
    get = (x < 3) | (half == 0)
    for dy, copies in finish:
        for when, copy in copies:
            pl.when(when)(copy.wait if dy == 0 else copy.wait_send)
    for dy in (1, 3, 2):
        from_y = (y + dy) % 4

        @pl.when(get)
        def _(from_y=from_y):
            here = out_ref.at[0, :, pl.ds(pl.multiple_of(from_y * main, LANES), main)]
            remote(here, here, send_out.at[0, 0], recv_out.at[0, from_y], device(1, 0)).wait_recv()

        @pl.when(get & (from_y == 3))
        def _(from_y=from_y):
            here = out_ref.at[0, :, pl.ds(4 * main, extra)]
            remote(here, here, send_out.at[1, 0], recv_out.at[1, from_y], device(1, 0)).wait_recv()


def per_device(s_real, s_imag, chan_l, counts, jlevel, allowed, recoup):
    rows, width = s_real.shape[1:]
    live, upper, main, extra, lower = plan(rows, width)
    table = recoup * allowed.astype(jnp.float32)
    meta = jnp.concatenate([
        chan_l, jnp.broadcast_to(counts[:, None], (1, LANES)), jnp.broadcast_to(jlevel[:, None], (1, LANES))], 1)
    vmem = pl.BlockSpec(memory_space=pltpu.VMEM)
    dma = pltpu.SemaphoreType.DMA
    return pl.pallas_call(
        functools.partial(kernel, rows, width),
        grid=(1,),
        out_shape=jax.ShapeDtypeStruct((1, rows, width), jnp.float32),
        in_specs=[vmem] * 4,
        out_specs=pl.BlockSpec(memory_space=pl.ANY),
        scratch_shapes=[
            pltpu.VMEM((14 * rows, upper), jnp.bfloat16),
            pltpu.VMEM((14 * rows, lower), jnp.bfloat16),
            pltpu.VMEM((2, 2 * rows, lower), jnp.bfloat16),
            pltpu.VMEM((2, upper, lower), jnp.float32),
            pltpu.VMEM((4, rows, lower), jnp.float32),
            pltpu.VMEM((4, rows, lower), jnp.float32),
            pltpu.VMEM((upper, lower), jnp.float32),
            pltpu.VMEM((rows, 2 * rows), jnp.float32),
            pltpu.VMEM((8, width + 2 * LANES), jnp.int32),
            dma((64,)), dma((7, 2)), dma((64,)), dma((7, 2)),
            dma((4,)), dma((4,)), dma((2, 4)), dma((2, 4)), dma((16,)),
        ],
        compiler_params=pltpu.CompilerParams(
            collective_id=0, has_side_effects=True, vmem_limit_bytes=48 << 20),
        cost_estimate=pl.CostEstimate(
            flops=16 * 7 * rows * upper * lower, bytes_accessed=8 * rows * width, transcendentals=0),
    )(s_real, s_imag, meta, table)


def solution(mesh):
    placed = (
        P("jpair", "row", None),
        P("jpair", "row", None),
        P("jpair", None),
        P("jpair"),
        P("jpair"),
        P(),
        P(),
    )
    return jax.shard_map(
        per_device, mesh=mesh, in_specs=placed, out_specs=P("jpair", "row", None), check_vma=False
    )
```

time: 364 us -> 114 us (0.31)
  waiting for transfers between devices: 313 us -> 0 us
  Pallas kernels: 0 us -> 107 us
  matrix products: 23.2 us -> 0 us
  between operations: 16.1 us -> 1.34 us
  other arithmetic: 5.49 us -> 1.47 us
  starting transfers between devices: 3.88 us -> 0 us
    reduce_scatter x1 -> x0, waiting for transfers between devices: 263 us -> none  [per_device(): lax.psum_scatter(lax.dot_general(left_side, right_side, (((0,), (0,)), ((...]
    pallas_call x0 -> x1, Pallas kernels: none -> 107 us  [per_device(): pl.pallas_call(functools.partial(kernel, rows, width), grid=(1,), out_sha...]
    ppermute x4 -> x0, waiting for transfers between devices: 50.8 us -> none  [partner(): return lax.ppermute(value, axis, pairs)]
    dot_general x3 -> x0, matrix products: 23.2 us -> none  [the longest x1 18.8 us: per_device(): lax.dot_general(left_side, right_side, (((0,), (0,)), ((), ())), preferre...]
    ppermute x4 -> x0, starting transfers between devices: 3.88 us -> none  [partner(): return lax.ppermute(value, axis, pairs)]
    select_n x4 -> x0, other arithmetic: 3.82 us -> none  [the longest x1 2.3 us: per_device(): mine_re = jnp.where(both_live, s_real[0], zeros_bf)]
  transfers between devices with their start and end apart: 5 -> 0, of which waited for: 4 -> 0; matrix products, arithmetic and copies ran while one was open for 1% -> 0% of each run, Pallas kernels for 0% -> 0%
where the time goes in v1:
time: 114 us
  Pallas kernels  107 us (94%)
  local copies, waits for them, and re-layouts  3.97 us (3%)
  other arithmetic  1.47 us (1%)
  between operations  1.34 us (1%)
    pallas_call x1, Pallas kernels, per_device(): pl.pallas_call(functools.partial(kernel, rows, width), grid=(1,), out_sha...  107 us
    unnamed x5, local copies, waits for them, and re-layouts  3.95 us

profile of v1, /device:TPU:1, one launch (start us, length us, event | category | flops | bytes accessed | tf_op | source)
XLA Modules:
  0.0 113.7 jit_solution(4248196637737479099)
XLA Ops:
  1.3 0.7 reshape_add_fusion.meta_ref
  2.1 0.7 convert_multiply_fusion.table_ref
  2.8 0.0 copy-start
  2.8 1.3 %copy-done = bf16[1,192,3072]{2,1,0:T(8,128)(2,1)S(1)} copy-done((bf16[1,192,3072]{2,1,0:T(8,128)(2,1)S(1)}, bf16[1,192,3072]{2,1,0:T(8,128)(2,1)}, u32[]{:S(2)}) %copy-start) | copy-done | bytes 1179672
  4.1 0.0 copy-start.1
  4.1 1.3 %copy-done.1 = bf16[1,192,3072]{2,1,0:T(8,128)(2,1)S(1)} copy-done((bf16[1,192,3072]{2,1,0:T(8,128)(2,1)S(1)}, bf16[1,192,3072]{2,1,0:T(8,128)(2,1)}, u32[]{:S(2)}) %copy-start.1) | copy-done | bytes 1179672
  5.4 106.9 %shard_map.73 = f32[1,192,3072]{2,1,0:T(8,128)S(1)} custom-call(bf16[1,192,3072]{2,1,0:T(8,128)(2,1)S(1)} %copy-done, bf16[1,192,3072]{2,1,0:T(8,128)(2,1)S(1)} %copy-done.1, s32[1,3328]{1,0:T(1,128)S(1)} %reshape_add_fusion.meta_ref, f32[32,32]{1,0:T(8,128)S(1)} %convert_multiply_fusion.table_ref), custom_call_target="tpu_custom_call" | custom-call | flops 12683575296 | bytes 4718592 | tf_op jit(solution)/shard_map/pallas_call | solution.py:345
  112.3 1.4 %copy.11 = f32[1,192,3072]{2,1,0:T(8,128)} copy(f32[1,192,3072]{2,1,0:T(8,128)S(1)} %shard_map.73) | data formatting | bytes 4718592
  (4 shorter events, 0.0 us)
Async XLA Ops:
  2.8 1.3 %copy-start = (bf16[1,192,3072]{2,1,0:T(8,128)(2,1)S(1)}, bf16[1,192,3072]{2,1,0:T(8,128)(2,1)}, u32[]{:S(2)}) copy-start(bf16[1,192,3072]{2,1,0:T(8,128)(2,1)} %re_ref.1) | copy-start | bytes 3538948
  4.1 1.3 %copy-start.1 = (bf16[1,192,3072]{2,1,0:T(8,128)(2,1)S(1)}, bf16[1,192,3072]{2,1,0:T(8,128)(2,1)}, u32[]{:S(2)}) copy-start(bf16[1,192,3072]{2,1,0:T(8,128)(2,1)} %im_ref.1) | copy-start | bytes 3538948

commit v2 on v1

--- a/solution.py
+++ b/solution.py
@@ -20,8 +20,8 @@
 
 
 def kernel(
-    rows, width, re_ref, im_ref, meta_ref, table_ref, out_ref,
-    up, low, swapped, acc, other, ready, weight, zeros, meta,
+    rows, width, re_ref, im_ref, chan_ref, count_ref, level_ref, allowed_ref, recoup_ref, out_ref,
+    up, low, swapped, acc, other, ready, weight, zeros, mine, theirs, labels,
     send_up, recv_up, send_low, recv_low, send_sum, recv_sum, send_out, recv_out, local_sem,
 ):
     live, upper, main, extra, lower = plan(rows, width)
@@ -50,8 +50,8 @@
     def slab_at(dx, dhalf):
         return 2 * ((x + dx) % 4) + (half + dhalf) % 2
 
-    def piece(buffer, slab, part):
-        return buffer.at[pl.ds(pl.multiple_of(slab * (2 * rows) + part * rows, rows), rows)]
+    def piece(buffer, slab, part, count):
+        return buffer.at[pl.ds(pl.multiple_of(slab * (2 * rows) + part * rows, rows), rows), pl.ds(0, count)]
 
     pending = []
 
@@ -59,54 +59,64 @@
         pl.when(when)(copy.start)
         pending.append((when, copy))
 
-    def arrived(when, buffer, sems, slab, part):
-        @pl.when(when)
-        def _():
-            here = piece(buffer, slab, part)
-            remote(here, here, send_up.at[0], sems.at[slab, part], device(1, 0)).wait_recv()
+    def arrived(when, buffer, slab, part):
+        here_up = buffer is up
+        sems = recv_up if here_up else recv_low
+        sizes = ((x < 3, upper), (x == 3, 2 * rows)) if here_up else ((y < 3, main), (y == 3, lower))
+        for size_when, count in sizes:
+            @pl.when(when & size_when)
+            def _(count=count):
+                here = piece(buffer, slab, part, count)
+                remote(here, here, send_up.at[0], sems.at[slab, part], device(1, 0)).wait_recv()
 
     my_slab = slab_at(0, 0)
     have_rows = my_slab < 7
     up_from = is_upper & have_rows
     low_from = is_lower & have_rows
 
-    partner = device(0, 1 - 2 * parity)
-    meta_copy = remote(meta_ref, meta.at[pl.ds(0, 1)], local_sem.at[0], local_sem.at[1], partner)
+    mine[:, :width] = chan_ref[...]
+    mine[:, width:width + LANES] = jnp.broadcast_to(count_ref[...], (1, LANES))
+    mine[:, width + LANES:] = jnp.broadcast_to(level_ref[...], (1, LANES))
+    meta_copy = remote(mine, theirs, local_sem.at[0], local_sem.at[1], device(0, 1 - 2 * parity))
     meta_copy.start()
 
+    def send_up_piece(when, to_x, src, part, n, slab, where):
+        for narrow, count in ((False, upper), (True, 2 * rows)):
+            send(when & ((to_x == 3) if narrow else (to_x < 3)), remote(
+                src(count), piece(up, slab, part, count), send_up.at[n], recv_up.at[slab, part], where))
+
+    def send_low_piece(when, to_y, src, part, n, slab, where):
+        for wide, count in ((False, main), (True, lower)):
+            send(when & ((to_y == 3) if wide else (to_y < 3)), remote(
+                src(count), piece(low, slab, part, count), send_low.at[n], recv_low.at[slab, part], where))
+
     def up_columns(part, to_x):
-        return source[part].at[0, :, pl.ds(pl.multiple_of(to_x * upper, LANES), upper)]
+        return lambda count: source[part].at[0, :, pl.ds(pl.multiple_of(to_x * upper, LANES), count)]
 
     def low_columns(part, to_y):
-        return source[part].at[0, :, pl.ds(pl.multiple_of(to_y * main, LANES), lower)]
+        return lambda count: source[part].at[0, :, pl.ds(pl.multiple_of(to_y * main, LANES), count)]
 
     for part in range(2):
         for n, dy in enumerate((1, 3)):
-            send(up_from, remote(
-                up_columns(part, x), piece(up, my_slab, part),
-                send_up.at[6 + 2 * n + part], recv_up.at[my_slab, part], device(0, dy)))
+            send_up_piece(up_from, x, up_columns(part, x), part, 6 + 2 * n + part, my_slab, device(0, dy))
     for n, dx in enumerate((1, 3, 2)):
         for part in range(2):
-            send(up_from, remote(
-                up_columns(part, (x + dx) % 4), piece(up, my_slab, part),
-                send_up.at[2 * n + part], recv_up.at[my_slab, part], device(dx, 0)))
+            to_x = (x + dx) % 4
+            send_up_piece(up_from, to_x, up_columns(part, to_x), part, 2 * n + part, my_slab, device(dx, 0))
     for n, dy in enumerate((1, 3, 2)):
         for part in range(2):
-            send(low_from, remote(
-                low_columns(part, (y + dy) % 4), piece(low, my_slab, part),
-                send_low.at[2 * n + part], recv_low.at[my_slab, part], device(0, dy)))
+            to_y = (y + dy) % 4
+            send_low_piece(low_from, to_y, low_columns(part, to_y), part, 2 * n + part, my_slab, device(0, dy))
     for part in range(2):
         for n, dx in enumerate((1, 3)):
-            send(low_from, remote(
-                low_columns(part, y), piece(low, my_slab, part),
-                send_low.at[6 + 2 * n + part], recv_low.at[my_slab, part], device(dx, 0)))
+            send_low_piece(low_from, y, low_columns(part, y), part, 6 + 2 * n + part, my_slab, device(dx, 0))
 
     own = []
     for part in range(2):
         own.append((up_from, pltpu.make_async_copy(
-            up_columns(part, x), piece(up, my_slab, part), local_sem.at[2 + part])))
+            up_columns(part, x)(upper), piece(up, my_slab, part, upper), local_sem.at[2 + part])))
         own.append((low_from, pltpu.make_async_copy(
-            low_columns(part, y), piece(low, my_slab, part), local_sem.at[2 + part])))
+            low_columns(part, y)(lower), piece(low, my_slab, part, lower), local_sem.at[2 + part])))
     for when, copy in own:
         pl.when(when)(copy.start)
 
@@ -122,20 +132,20 @@
     acc[...] = jnp.zeros_like(acc)
 
     meta_copy.wait()
-    mine, theirs = meta_ref[...], meta[0:1, :]
-    first = jnp.where(is_upper, mine, theirs)
-    second = jnp.where(is_upper, theirs, mine)
+    first = jnp.where(is_upper, mine[...], theirs[...])
+    second = jnp.where(is_upper, theirs[...], mine[...])
     upper_count, lower_count = first[:, width:width + 1], second[:, width:width + 1]
     upper_deg = (2 * first[:, width + LANES:width + LANES + 1] + 1).astype(jnp.float32)
     lower_deg = (2 * second[:, width + LANES:width + LANES + 1] + 1).astype(jnp.float32)
     factor = 2.0 * lower_deg / (upper_deg + lower_deg)
-    meta[1:2, :] = first
-    meta[2:3, :] = second
-    levels = table_ref.shape[0]
+    labels[0:1, :] = first
+    labels[1:2, :] = second
+    table = recoup_ref[...] * allowed_ref[...].astype(jnp.float32)
+    levels = table.shape[0]
     c_start = pl.multiple_of(x * upper, LANES)
     d_start = pl.multiple_of(y * main, LANES)
-    c_labels = meta[1:2, pl.ds(c_start, upper)]
-    d_labels = meta[2:3, pl.ds(d_start, lower)]
+    c_labels = labels[0:1, pl.ds(c_start, upper)]
+    d_labels = labels[1:2, pl.ds(d_start, lower)]
     c_open = c_start + lax.broadcasted_iota(jnp.int32, (1, upper), 1) < upper_count
     d_open = d_start + lax.broadcasted_iota(jnp.int32, (1, lower), 1) < lower_count
     c_labels = jnp.where(c_open, c_labels, -1)
@@ -143,7 +153,7 @@
     c_hot = (lax.broadcasted_iota(jnp.int32, (levels, upper), 0) == c_labels).astype(jnp.float32)
     d_hot = (lax.broadcasted_iota(jnp.int32, (levels, lower), 0) == d_labels).astype(jnp.float32)
     picked = factor * jnp.dot(
-        table_ref[...], d_hot, precision=lax.Precision.HIGHEST, preferred_element_type=jnp.float32)
+        table, d_hot, precision=lax.Precision.HIGHEST, preferred_element_type=jnp.float32)
     weight[...] = lax.dot_general(
         c_hot, picked, (((0,), (0,)), ((), ())),
         precision=lax.Precision.HIGHEST, preferred_element_type=jnp.float32)
@@ -178,88 +188,99 @@
     used = {"up": 10, "low": 10}
 
     def on_up(when, slab, part, dy):
-        n = used["up"]
+        send_up_piece(when, x, lambda count: piece(up, slab, part, count), part, used["up"], slab, device(0, dy))
         used["up"] += 1
-        here = piece(up, slab, part)
-        send(when, remote(here, here, send_up.at[n], recv_up.at[slab, part], device(0, dy)))
 
     def on_low(when, slab, part, dx):
-        n = used["low"]
+        send_low_piece(when, y, lambda count: piece(low, slab, part, count), part, used["low"], slab, device(dx, 0))
         used["low"] += 1
-        here = piece(low, slab, part)
-        send(when, remote(here, here, send_low.at[n], recv_low.at[slab, part], device(dx, 0)))
 
     def own_low(dhalf):
         slab = slab_at(0, dhalf)
         when = (is_upper if dhalf == 0 else (slab >= 0)) & (slab < 7)
         for part in range(2):
-            arrived(when, low, recv_low, slab, part)
+            arrived(when, low, slab, part)
             for dx in (1, 3):
                 on_low(when, slab, part, dx)
 
-    def next_low(dx, dhalf):
+    def next_low(side, dx, dhalf):
         slab = slab_at(dx, dhalf)
-        when = slab < 7
+        when = side & (slab < 7)
         first_part = 0 if dx == 3 else 1
         for part in (first_part, 1 - first_part):
-            arrived(when, low, recv_low, slab, part)
+            arrived(when, low, slab, part)
             if part == first_part:
                 on_low(when, slab, part, 4 - dx)
 
     def far_low(dhalf):
         slab = slab_at(2, dhalf)
         for part in range(2):
-            arrived(slab < 7, low, recv_low, slab, part)
+            arrived(slab < 7, low, slab, part)
 
     def even_up(dx):
         slab = slab_at(dx, 0)
         when = is_upper & (slab < 7)
         for part in range(2):
-            arrived(when, up, recv_up, slab, part)
+            arrived(when, up, slab, part)
             for dy in (1, 3):
-                on_up(when, slab, part, dy)
+                on_up(when if dy == 1 + 2 * part else when & (slab < 6), slab, part, dy)
 
     def odd_up(dx):
-        for dy, dhalf in ((3, 0), (1, 1)):
+        for dy, dhalf, part in ((3, 0, 0), (1, 1, 1)):
             slab = slab_at(dx, dhalf)
             when = is_lower & (slab < 7)
-            first_part = 0 if dy == 3 else 1
-            for part in (first_part, 1 - first_part):
-                arrived(when, up, recv_up, slab, part)
-                if part == first_part:
-                    on_up(when, slab, part, 4 - dy)
+            arrived(when, up, slab, part)
+            on_up(when, slab, part, 4 - dy)
+
+    def odd_rest(dx, dhalf):
+        slab = slab_at(dx, dhalf)
+        arrived(is_lower & (slab < 7), up, slab, 1 - dhalf)
 
     def far_up(dx):
         slab = slab_at(dx, 1)
         for part in range(2):
-            arrived(is_upper & (slab < 7), up, recv_up, slab, part)
+            arrived(is_upper & (slab < 7), up, slab, part)
+            if dx != 0:
+                on_up(is_upper & (slab == 6), slab, part, 1 + 2 * part)
 
     odd_up(0)
     own_low(0)
     own_low(1)
-    accumulate(slab_at(0, 0))
+    next_low(is_lower, 1, 0)
+    next_low(is_lower, 3, 0)
     even_up(1)
     even_up(3)
-    next_low(1, 0)
-    next_low(3, 0)
-    next_low(1, 1)
-    next_low(3, 1)
+    odd_rest(0, 0)
+    accumulate(slab_at(0, 0))
     odd_up(1)
     odd_up(3)
     even_up(2)
     far_up(0)
+    next_low(is_upper, 1, 0)
+    next_low(is_upper, 3, 0)
+    next_low(is_lower, 1, 1)
+    next_low(is_lower, 3, 1)
+    odd_rest(0, 1)
     accumulate(slab_at(0, 1))
+    odd_rest(1, 0)
     accumulate(slab_at(1, 0))
+    odd_rest(3, 0)
     accumulate(slab_at(3, 0))
+    next_low(is_upper, 1, 1)
+    next_low(is_upper, 3, 1)
     odd_up(2)
     far_up(1)
+    odd_rest(1, 1)
     accumulate(slab_at(1, 1))
     far_up(3)
+    odd_rest(3, 1)
     accumulate(slab_at(3, 1))
     far_low(0)
+    odd_rest(2, 0)
     accumulate(slab_at(2, 0))
     far_low(1)
     far_up(2)
+    odd_rest(2, 1)
     accumulate(slab_at(2, 1))
 
     order = (2, 1, 3, 0)
@@ -275,11 +296,6 @@
             acc.at[to_y % 2, rows_of(to_y, 1 - core)], other.at[n], send_sum.at[n], recv_sum.at[n], device(0, 0, 1))
         pl.when(when)(copy.start)
         sums.append((when, copy))
-
-    def out_copy(n, dy, start, count, sems, last):
-        dst = out_ref.at[0, :, pl.ds(start, count)]
-        src = ready.at[n, :, pl.ds(last, count)]
-        return src, dst
 
     finish = []
     for n, dy in enumerate(order):
@@ -337,16 +353,13 @@
 def per_device(s_real, s_imag, chan_l, counts, jlevel, allowed, recoup):
     rows, width = s_real.shape[1:]
     live, upper, main, extra, lower = plan(rows, width)
-    table = recoup * allowed.astype(jnp.float32)
-    meta = jnp.concatenate([
-        chan_l, jnp.broadcast_to(counts[:, None], (1, LANES)), jnp.broadcast_to(jlevel[:, None], (1, LANES))], 1)
     vmem = pl.BlockSpec(memory_space=pltpu.VMEM)
     dma = pltpu.SemaphoreType.DMA
     return pl.pallas_call(
         functools.partial(kernel, rows, width),
         grid=(1,),
         out_shape=jax.ShapeDtypeStruct((1, rows, width), jnp.float32),
-        in_specs=[vmem] * 4,
+        in_specs=[pl.BlockSpec(memory_space=pl.ANY)] * 2 + [vmem] * 5,
         out_specs=pl.BlockSpec(memory_space=pl.ANY),
         scratch_shapes=[
             pltpu.VMEM((14 * rows, upper), jnp.bfloat16),
@@ -357,15 +370,17 @@
             pltpu.VMEM((4, rows, lower), jnp.float32),
             pltpu.VMEM((upper, lower), jnp.float32),
             pltpu.VMEM((rows, 2 * rows), jnp.float32),
+            pltpu.VMEM((1, width + 2 * LANES), jnp.int32),
+            pltpu.VMEM((1, width + 2 * LANES), jnp.int32),
             pltpu.VMEM((8, width + 2 * LANES), jnp.int32),
             dma((64,)), dma((7, 2)), dma((64,)), dma((7, 2)),
             dma((4,)), dma((4,)), dma((2, 4)), dma((2, 4)), dma((16,)),
         ],
         compiler_params=pltpu.CompilerParams(
-            collective_id=0, has_side_effects=True, vmem_limit_bytes=48 << 20),
+            collective_id=0, has_side_effects=True, vmem_limit_bytes=60 << 20),
         cost_estimate=pl.CostEstimate(
             flops=16 * 7 * rows * upper * lower, bytes_accessed=8 * rows * width, transcendentals=0),
-    )(s_real, s_imag, meta, table)
+    )(s_real, s_imag, chan_l, counts[:, None], jlevel[:, None], allowed, recoup)
 
 
 def solution(mesh):

time: 114 us -> 109 us (0.956)
  the two profiles are of different devices: /device:TPU:1 before, /device:TPU:51 now
where the time goes in v2:
time: 109 us
  Pallas kernels  105 us (96%)
  local copies, waits for them, and re-layouts  3.3 us (3%)
  between operations  1.3 us (1%)
    pallas_call x1, Pallas kernels, per_device(): pl.pallas_call(functools.partial(kernel, rows, width), grid=(1,), out_sha...  105 us
    unnamed x1, local copies, waits for them, and re-layouts  3.3 us

profile of v2, /device:TPU:51, one launch (start us, length us, event | category | flops | bytes accessed | tf_op | source)
XLA Modules:
  0.0 109.2 jit_solution(18336231450492093105)
XLA Ops:
  1.3 104.6 %shard_map.73 = f32[1,192,3072]{2,1,0:T(8,128)} custom-call(bf16[1,192,3072]{2,1,0:T(8,128)(2,1)} %re_ref.1, bf16[1,192,3072]{2,1,0:T(8,128)(2,1)} %im_ref.1, s32[1,3072]{1,0:T(1,128)} %chan_ref.1, s32[1,1]{1,0:T(1,128)} %bitcast.2.count_ref, s32[1,1]{1,0:T(1,128)} %bitcast.3.level_ref, s32[32,32]{1,0:T(8,128)} %allowed_ref.1, f32[32,32]{1,0:T(8,128)} %recoup_ref.1), custom_call_target="tpu_custom_call" | custom-call | flops 12683575296 | bytes 4718592 | tf_op jit(solution)/shard_map/pallas_call | solution.py:358
  105.9 3.3 %copy.11 = f32[1,192,3072]{2,1,0:T(8,128)} copy(f32[1,192,3072]{2,1,0:T(8,128)} %shard_map.73) | data formatting | bytes 4718592

commit v3 on v2

v3 whole, which is shorter than its diff:
```python
import functools

import jax
import jax.numpy as jnp
from jax import lax
from jax.experimental import pallas as pl
from jax.experimental.pallas import tpu as pltpu
from jax.sharding import PartitionSpec as P

MESH = pl.DeviceIdType.MESH
LANES = 128
RELAY, UPPER, LOWER, SUM = range(4)
ORDER = (
    (
        (RELAY, 0), (RELAY, 1), (UPPER, 1, 0, 0), (UPPER, 3, 0, 0), (LOWER, 0, 1, 0), (LOWER, 0, 0, 0),
        (UPPER, 1, 0, 1), (LOWER, 0, 1, 1), (LOWER, 0, 0, 1), (SUM, 0, 0), (UPPER, 3, 0, 1), (SUM, 0, 1),
        (UPPER, 2, 0, 0), (LOWER, 3, 1, 0), (LOWER, 3, 0, 0), (UPPER, 2, 0, 1), (LOWER, 1, 1, 1), (SUM, 3, 1),
        (LOWER, 1, 0, 1), (SUM, 1, 0), (SUM, 3, 0), (SUM, 1, 1), (SUM, 2, 1), (SUM, 2, 0),
    ),
    (
        (LOWER, 3, 0, 0), (UPPER, 0, 0, 0), (UPPER, 0, 1, 1), (LOWER, 1, 0, 1), (LOWER, 0, 1, 0), (LOWER, 0, 1, 1),
        (SUM, 0, 1), (UPPER, 1, 0, 0), (LOWER, 3, 1, 0), (UPPER, 1, 1, 1), (UPPER, 3, 0, 0), (LOWER, 1, 1, 1),
        (SUM, 1, 1), (SUM, 1, 0), (UPPER, 3, 1, 1), (SUM, 3, 0), (SUM, 3, 1), (UPPER, 2, 0, 0), (UPPER, 2, 1, 1),
        (SUM, 0, 0), (SUM, 2, 0), (SUM, 2, 1),
    ),
    (
        (RELAY, 1), (RELAY, 0), (UPPER, 1, 0, 0), (UPPER, 3, 0, 0), (LOWER, 0, 0, 0), (LOWER, 0, 1, 0),
        (UPPER, 1, 0, 1), (UPPER, 3, 0, 1), (LOWER, 0, 0, 1), (SUM, 0, 0), (LOWER, 0, 1, 1), (UPPER, 0, 1, 1),
        (UPPER, 0, 1, 0), (SUM, 0, 1), (UPPER, 2, 0, 0), (LOWER, 3, 0, 0), (LOWER, 1, 0, 1), (SUM, 1, 0),
        (LOWER, 3, 1, 0), (UPPER, 2, 0, 1), (LOWER, 1, 1, 1), (SUM, 3, 0), (SUM, 1, 1), (SUM, 3, 1), (SUM, 2, 0),
        (SUM, 2, 1),
    ),
    (
        (UPPER, 0, 0, 0), (UPPER, 0, 1, 1), (LOWER, 3, 0, 0), (SUM, 0, 0), (LOWER, 1, 0, 1), (LOWER, 0, 1, 1),
        (LOWER, 0, 1, 0), (UPPER, 1, 1, 1), (UPPER, 1, 0, 0), (UPPER, 3, 0, 0), (UPPER, 3, 1, 1), (SUM, 1, 0),
        (LOWER, 3, 1, 0), (SUM, 3, 0), (UPPER, 2, 0, 0), (LOWER, 1, 1, 1), (SUM, 1, 1), (SUM, 3, 1),
        (UPPER, 2, 1, 1), (SUM, 0, 1), (SUM, 2, 0), (SUM, 2, 1),
    ),
)


def plan(rows, width):
    live = 14 * rows
    upper = 4 * rows
    main = live // LANES // 4 * LANES
    extra = live - 4 * main
    return live, upper, main, extra, main + extra


def kernel(
    rows, width, re_ref, im_ref, chan_ref, count_ref, level_ref, allowed_ref, recoup_ref, out_ref,
    up, low, transit, swapped, acc, other, coded, got, gain, got_gain, weight, mine, theirs, labels,
    send_up, recv_up, send_low, recv_low, recv_transit, send_sum, recv_sum, send_out, recv_out, local_sem,
):
    live, upper, main, extra, lower = plan(rows, width)
    j, r = lax.axis_index("jpair"), lax.axis_index("row")
    pair, parity = j // 2, j % 2
    x, half, core = r // 4, (r // 2) % 2, r % 2
    y = 2 * half + parity
    is_upper, is_lower = parity == 0, parity == 1
    source = (re_ref, im_ref)

    def device(dx, dy, dcore=0):
        to_x, to_y = (x + dx) % 4, (y + dy) % 4
        return (2 * pair + to_y % 2, 4 * to_x + 2 * (to_y // 2) + (core + dcore) % 2)

    def remote(src, dst, send, recv, where):
        return pltpu.make_async_remote_copy(
            src_ref=src, dst_ref=dst, send_sem=send, recv_sem=recv, device_id=where, device_id_type=MESH
        )

    barrier = pltpu.get_barrier_semaphore()
    greeted = [(1, 0, 0), (3, 0, 0), (2, 0, 0), (0, 1, 0), (0, 3, 0), (0, 2, 0), (0, 0, 1)]
    for offset in greeted:
        pl.semaphore_signal(barrier, inc=1, device_id=device(*offset), device_id_type=MESH)
    pl.semaphore_wait(barrier, len(greeted))

    def slab_at(dx, dhalf):
        return 2 * ((x + dx) % 4) + (half + dhalf) % 2

    def piece(buffer, slab, part, count):
        return buffer.at[pl.ds(pl.multiple_of(slab * (2 * rows) + part * rows, rows), rows), pl.ds(0, count)]

    my_slab = slab_at(0, 0)
    have_rows = my_slab < 7
    up_from, low_from = is_upper & have_rows, is_lower & have_rows

    mine[:, :width] = chan_ref[...]
    mine[:, width:width + LANES] = jnp.broadcast_to(count_ref[...], (1, LANES))
    mine[:, width + LANES:] = jnp.broadcast_to(level_ref[...], (1, LANES))
    meta_copy = remote(mine, theirs, local_sem.at[0], local_sem.at[1], device(0, 1 - 2 * parity))
    meta_copy.start()

    def low_count(to_y):
        return lower if to_y % 4 == 3 else main

    def up_columns(part, to_x):
        return lambda count: source[part].at[0, :, pl.ds(pl.multiple_of(to_x * upper, LANES), count)]

    def low_columns(part, to_y, count):
        return source[part].at[0, :, pl.ds(pl.multiple_of(to_y * main, LANES), count)]

    pending = [[] for _ in range(4)]
    used = {"up": 0, "low": 0}

    def send(at_y, make):
        for when, copy in make():
            pl.when(when)(copy.start)
        pending[at_y].append(make)

    def send_up_piece(at_y, when, src, part, dx, dhalf, to):
        n = used["up"]
        used["up"] += 1

        def make():
            slab = slab_at(dx, dhalf)
            ok = (slab < 7) if when is None else (slab < 7) & when()
            to_x = (x + to[0]) % 4
            return [
                (ok & size_when, remote(
                    src(slab, count), piece(up, slab, part, count), send_up.at[n], recv_up.at[slab, part], device(*to)))
                for size_when, count in ((to_x < 3, upper), (to_x == 3, 2 * rows))]

        send(at_y, make)

    def send_low_piece(at_y, src, part, dx, dhalf, to, count, passing=False):
        n = used["low"]
        used["low"] += 1

        def make():
            slab = slab_at(dx, dhalf)
            if passing:
                dst, recv = transit.at[pl.ds(part * rows, rows), pl.ds(0, count)], recv_transit.at[part]
            else:
                dst, recv = piece(low, slab, part, count), recv_low.at[slab, part]
            return [(slab < 7, remote(src(slab), dst, send_low.at[n], recv, device(*to)))]

        send(at_y, make)

    def begin(at_y):
        used["up"] = used["low"] = 0
        if at_y % 2 == 0:
            for part, dy in ((0, 1), (1, 3), (0, 3), (1, 1)):
                when = (lambda: x == 3) if at_y == 0 and dy != 1 + 2 * part else None
                send_up_piece(at_y, when, lambda slab, count, part=part: up_columns(part, x)(count), part, 0, 0, (0, dy))
            for dx in (1, 3, 2):
                for part in range(2):
                    send_up_piece(
                        at_y, None, lambda slab, count, part=part, dx=dx: up_columns(part, (x + dx) % 4)(count),
                        part, 0, 0, (dx, 0))
        else:
            to = [(0, part, 1 + 2 * part, at_y + 2) for part in range(2)]
            to += [(0, part, dy, at_y + dy) for part in range(2) for dy in (1, 3)]
            to += [(dx, part, 0, at_y) for part in range(2) for dx in (1, 3)]
            for n, (dx, part, dy, to_y) in enumerate(to):
                count = low_count(to_y)
                send_low_piece(
                    at_y, lambda slab, part=part, to_y=to_y, count=count: low_columns(part, to_y % 4, count),
                    part, 0, 0, (dx, dy), count, passing=n < 2)
        marks.append(dict(used))

    marks = []
    for at_y in range(4):
        pl.when(y == at_y)(functools.partial(begin, at_y))

    own = []
    for part in range(2):
        own.append((up_from, pltpu.make_async_copy(
            up_columns(part, x)(upper), piece(up, my_slab, part, upper), local_sem.at[2 + part])))
        own.append((low_from, pltpu.make_async_copy(
            low_columns(part, y, lower), piece(low, my_slab, part, lower), local_sem.at[2 + part])))
    for when, copy in own:
        pl.when(when)(copy.start)

    out_ref[0, :, live:] = jnp.zeros((rows, width - live), jnp.float32)

    @pl.when(my_slab == 7)
    def _():
        out_ref[0, :, :live] = jnp.zeros((rows, live), jnp.float32)

    acc[...] = jnp.zeros_like(acc)

    meta_copy.wait()
    first = jnp.where(is_upper, mine[...], theirs[...])
    second = jnp.where(is_upper, theirs[...], mine[...])
    upper_count, lower_count = first[:, width:width + 1], second[:, width:width + 1]
    upper_deg = (2 * first[:, width + LANES:width + LANES + 1] + 1).astype(jnp.float32)
    lower_deg = (2 * second[:, width + LANES:width + LANES + 1] + 1).astype(jnp.float32)
    factor = 2.0 * lower_deg / (upper_deg + lower_deg)
    labels[0:1, :] = first
    labels[1:2, :] = second
    table = recoup_ref[...] * allowed_ref[...].astype(jnp.float32)
    levels = table.shape[0]
    c_start = pl.multiple_of(x * upper, LANES)
    d_start = pl.multiple_of(y * main, LANES)
    c_labels = labels[0:1, pl.ds(c_start, upper)]
    d_labels = labels[1:2, pl.ds(d_start, lower)]
    c_open = c_start + lax.broadcasted_iota(jnp.int32, (1, upper), 1) < upper_count
    d_open = d_start + lax.broadcasted_iota(jnp.int32, (1, lower), 1) < lower_count
    c_labels = jnp.where(c_open, c_labels, -1)
    d_labels = jnp.where(d_open, d_labels, -1)
    c_hot = (lax.broadcasted_iota(jnp.int32, (levels, upper), 0) == c_labels).astype(jnp.float32)
    d_hot = (lax.broadcasted_iota(jnp.int32, (levels, lower), 0) == d_labels).astype(jnp.float32)
    picked = factor * jnp.dot(
        table, d_hot, precision=lax.Precision.HIGHEST, preferred_element_type=jnp.float32)
    weight[...] = lax.dot_general(
        c_hot, picked, (((0,), (0,)), ((), ())),
        precision=lax.Precision.HIGHEST, preferred_element_type=jnp.float32)
    least = jnp.minimum(upper_count, lower_count)
    for when, copy in own:
        pl.when(when)(copy.wait)

    tile = min(256, upper)

    def accumulate(slab):
        @pl.when(slab < 7)
        def _():
            row = pl.multiple_of(slab * 2 * rows, rows)
            first_row = (slab // 2) * (4 * rows) + (slab % 2) * (2 * rows) + core * rows
            row_ids = first_row + lax.broadcasted_iota(jnp.int32, (rows, lower), 0)
            keep = (row_ids < least).astype(jnp.float32).astype(jnp.bfloat16)
            low_re = low[pl.ds(row, rows)] * keep
            low_im = low[pl.ds(pl.multiple_of(row + rows, rows), rows)] * keep
            swapped[0, :rows] = low_re
            swapped[0, rows:] = low_im
            swapped[1, :rows] = low_im
            swapped[1, rows:] = -low_re

            @pl.loop(0, upper // tile)
            def _(n):
                start = pl.multiple_of(n * tile, tile)
                left = up[pl.ds(row, 2 * rows), pl.ds(start, tile)]
                for part in range(2):
                    acc[part, pl.ds(start, tile)] += lax.dot_general(
                        left, swapped[part], (((0,), (0,)), ((), ())), preferred_element_type=jnp.float32)

    def wait_piece(at_y, kind, slab, part):
        if kind == UPPER:
            for size_when, count in ((x < 3, upper), (x == 3, 2 * rows)):
                here = piece(up, slab, part, count)
                pl.when((slab < 7) & size_when)(
                    remote(here, here, send_up.at[0], recv_up.at[slab, part], device(1, 0)).wait_recv)
        else:
            here = piece(low, slab, part, low_count(at_y))
            pl.when(slab < 7)(remote(here, here, send_low.at[0], recv_low.at[slab, part], device(1, 0)).wait_recv)

    def go_on(at_y, kind, dx, dhalf, part):
        if kind == LOWER:
            count = low_count(at_y)
            for to_dx in ((1, 3) if dx == 0 else (4 - dx,)):
                send_low_piece(
                    at_y, lambda slab: piece(low, slab, part, count), part, dx, dhalf, (to_dx, 0), count)
            return
        when = None
        if at_y % 2 == 1:
            hops = [(part, 1 + 2 * part)]
        elif dhalf == 1:
            hops = [(part, 1 + 2 * part)]
            when = lambda: x < 3
        elif part == 0:
            hops = [(0, 1)]
        else:
            hops = [(1, 3), (0, 3), (1, 1)]
        for of_part, dy in hops:
            send_up_piece(
                at_y, when, lambda slab, count, of_part=of_part: piece(up, slab, of_part, count),
                of_part, dx, dhalf, (0, dy))

    def relay(at_y, part):
        dy = 1 + 2 * part
        count = low_count(at_y + dy)
        here = transit.at[pl.ds(part * rows, rows), pl.ds(0, count)]
        pl.when(slab_at(0, 1 - part) < 7)(
            remote(here, here, send_low.at[0], recv_transit.at[part], device(1, 0)).wait_recv)
        send_low_piece(at_y, lambda slab: here, part, 0, 1 - part, (0, dy), count)

    def steps(at_y):
        cut = [[]]
        for event in ORDER[at_y]:
            cut[-1].append(event)
            if event[0] == SUM:
                cut.append([])
        return cut

    waited = [{(UPPER if at_y % 2 == 0 else LOWER, 0, 0, part) for part in range(2)} for at_y in range(4)]

    def react(at_y, events):
        used.update(marks[at_y])
        for kind, *where in events:
            if kind == RELAY:
                relay(at_y, *where)
            elif kind == SUM:
                for piece_kind in (UPPER, LOWER):
                    for part in range(2):
                        key = (piece_kind, *where, part)
                        if key not in waited[at_y]:
                            wait_piece(at_y, piece_kind, slab_at(*where), part)
                        waited[at_y].add(key)
            else:
                wait_piece(at_y, kind, slab_at(*where[:2]), where[2])
                waited[at_y].add((kind, *where))
                go_on(at_y, kind, *where)
        marks[at_y] = dict(used)

    for n in range(8):
        slab = my_slab * 0
        for at_y in range(4):
            events = steps(at_y)[n]
            pl.when(y == at_y)(functools.partial(react, at_y, events))
            slab = jnp.where(y == at_y, slab_at(*events[-1][1:]), slab)
        accumulate(slab)

    order = (2, 1, 3, 0)

    def rows_of(to_y, of_core):
        return pl.ds(pl.multiple_of((to_y // 2) * (2 * rows) + of_core * rows, rows), rows)

    sums = []
    for n, dy in enumerate(order):
        to_y = (y + dy) % 4
        when = (x < 3) | (to_y < 2)
        copy = remote(
            acc.at[to_y % 2, rows_of(to_y, 1 - core)], other.at[n], send_sum.at[n], recv_sum.at[n], device(0, 0, 1))
        pl.when(when)(copy.start)
        sums.append((when, copy))

    def out_counts(of_y):
        return ((of_y < 3, main), (of_y == 3, lower))

    outs = []
    for n, dy in enumerate(order):
        to_y = (y + dy) % 4
        when, copy = sums[n]

        @pl.when(when)
        def _(n=n, dy=dy, to_y=to_y, copy=copy):
            copy.wait_recv()
            keep = rows_of(to_y, core)
            value = weight[keep] * (acc[to_y % 2, keep] + other[n])
            if dy == 0:
                for size_when, count in out_counts(y):
                    @pl.when(size_when)
                    def _(count=count):
                        out_ref[0, :, pl.ds(d_start, count)] = value[:, :count]
            else:
                largest = jnp.max(jnp.abs(value), axis=0, keepdims=True)
                unit = jnp.where(largest > 0.0, 1.0 / largest, 0.0)
                coded[n] = jnp.round(value * unit * 32767.0).astype(jnp.int32).astype(jnp.int16)
                gain[n] = largest

        if dy != 0:
            copies = [(when, remote(gain.at[n], got_gain.at[y], send_out.at[1, n], recv_out.at[1, y], device(0, dy)))]
            for size_when, count in out_counts(y):
                copies.append((when & size_when, remote(
                    coded.at[n, :, pl.ds(0, count)], got.at[:, pl.ds(d_start, count)],
                    send_out.at[0, n], recv_out.at[0, y], device(0, dy))))
            for start_when, out in copies:
                pl.when(start_when)(out.start)
            outs += copies

    have_out = (x < 3) | (half == 0)
    for dy in (1, 3, 2):
        from_y = (y + dy) % 4

        @pl.when(have_out)
        def _(from_y=from_y):
            remote(got_gain.at[from_y], got_gain.at[from_y], send_out.at[1, 0], recv_out.at[1, from_y], device(1, 0)).wait_recv()

        for size_when, count in out_counts(from_y):
            @pl.when(have_out & size_when)
            def _(from_y=from_y, count=count):
                columns = pl.ds(pl.multiple_of(from_y * main, LANES), count)
                here = got.at[:, columns]
                remote(here, here, send_out.at[0, 0], recv_out.at[0, from_y], device(1, 0)).wait_recv()
                value = got[:, columns].astype(jnp.int32).astype(jnp.float32) * (1.0 / 32767.0)
                out_ref[0, :, columns] = value * got_gain[from_y][:, :count]

    for at_y in range(4):
        @pl.when(y == at_y)
        def _(at_y=at_y):
            for make in pending[at_y]:
                for when, copy in make():
                    pl.when(when)(copy.wait_send)
    for when, copy in sums + outs:
        pl.when(when)(copy.wait_send)


def per_device(s_real, s_imag, chan_l, counts, jlevel, allowed, recoup):
    rows, width = s_real.shape[1:]
    live, upper, main, extra, lower = plan(rows, width)
    vmem = pl.BlockSpec(memory_space=pltpu.VMEM)
    dma = pltpu.SemaphoreType.DMA
    return pl.pallas_call(
        functools.partial(kernel, rows, width),
        grid=(1,),
        out_shape=jax.ShapeDtypeStruct((1, rows, width), jnp.float32),
        in_specs=[pl.BlockSpec(memory_space=pltpu.HBM)] * 2 + [vmem] * 5,
        out_specs=vmem,
        scratch_shapes=[
            pltpu.VMEM((14 * rows, upper), jnp.bfloat16),
            pltpu.VMEM((14 * rows, lower), jnp.bfloat16),
            pltpu.VMEM((2 * rows, lower), jnp.bfloat16),
            pltpu.VMEM((2, 2 * rows, lower), jnp.bfloat16),
            pltpu.VMEM((2, upper, lower), jnp.float32),
            pltpu.VMEM((4, rows, lower), jnp.float32),
            pltpu.VMEM((4, rows, lower), jnp.int16),
            pltpu.VMEM((rows, live), jnp.int16),
            pltpu.VMEM((4, 1, lower), jnp.float32),
            pltpu.VMEM((4, 1, lower), jnp.float32),
            pltpu.VMEM((upper, lower), jnp.float32),
            pltpu.VMEM((1, width + 2 * LANES), jnp.int32),
            pltpu.VMEM((1, width + 2 * LANES), jnp.int32),
            pltpu.VMEM((8, width + 2 * LANES), jnp.int32),
            dma((40,)), dma((7, 2)), dma((40,)), dma((7, 2)), dma((2,)),
            dma((4,)), dma((4,)), dma((2, 4)), dma((2, 4)), dma((8,)),
        ],
        compiler_params=pltpu.CompilerParams(
            collective_id=0, has_side_effects=True, vmem_limit_bytes=61 << 20),
        cost_estimate=pl.CostEstimate(
            flops=16 * 7 * rows * upper * lower, bytes_accessed=8 * rows * width, transcendentals=0),
    )(s_real, s_imag, chan_l, counts[:, None], jlevel[:, None], allowed, recoup)


def solution(mesh):
    placed = (
        P("jpair", "row", None),
        P("jpair", "row", None),
        P("jpair", None),
        P("jpair"),
        P("jpair"),
        P(),
        P(),
    )
    return jax.shard_map(
        per_device, mesh=mesh, in_specs=placed, out_specs=P("jpair", "row", None), check_vma=False
    )
```

time: 109 us -> 88.3 us (0.81)
  the two profiles are of different devices: /device:TPU:51 before, /device:TPU:1 now
where the time goes in v3:
time: 88.3 us; the launch traced here: 88.1 us
  Pallas kernels  83.5 us (95%)
  local copies, waits for them, and re-layouts  3.3 us (4%)
  between operations  1.3 us (1%)
    pallas_call x1, Pallas kernels, per_device(): pl.pallas_call(functools.partial(kernel, rows, width), grid=(1,), out_sha...  83.5 us
    unnamed x1, local copies, waits for them, and re-layouts  3.3 us

profile of v3, /device:TPU:1, one launch (start us, length us, event | category | flops | bytes accessed | tf_op | source)
XLA Modules:
  0.0 88.1 jit_solution(9360785637329417820)
XLA Ops:
  1.3 83.5 %shard_map.73 = f32[1,192,3072]{2,1,0:T(8,128)} custom-call(bf16[1,192,3072]{2,1,0:T(8,128)(2,1)} %re_ref.1, bf16[1,192,3072]{2,1,0:T(8,128)(2,1)} %im_ref.1, s32[1,3072]{1,0:T(1,128)} %chan_ref.1, s32[1,1]{1,0:T(1,128)} %bitcast.2.count_ref, s32[1,1]{1,0:T(1,128)} %bitcast.3.level_ref, s32[32,32]{1,0:T(8,128)} %allowed_ref.1, f32[32,32]{1,0:T(8,128)} %recoup_ref.1), custom_call_target="tpu_custom_call" | custom-call | flops 12683575296 | bytes 4718592 | tf_op jit(solution)/shard_map/pallas_call | solution.py:393
  84.8 3.3 %copy.11 = f32[1,192,3072]{2,1,0:T(8,128)} copy(f32[1,192,3072]{2,1,0:T(8,128)} %shard_map.73) | data formatting | bytes 4718592

commit v4 on v3

--- a/solution.py
+++ b/solution.py
@@ -13,28 +13,31 @@
 ORDER = (
     (
         (RELAY, 0), (RELAY, 1), (UPPER, 1, 0, 0), (UPPER, 3, 0, 0), (LOWER, 0, 1, 0), (LOWER, 0, 0, 0),
-        (UPPER, 1, 0, 1), (LOWER, 0, 1, 1), (LOWER, 0, 0, 1), (SUM, 0, 0), (UPPER, 3, 0, 1), (SUM, 0, 1),
-        (UPPER, 2, 0, 0), (LOWER, 3, 1, 0), (LOWER, 3, 0, 0), (UPPER, 2, 0, 1), (LOWER, 1, 1, 1), (SUM, 3, 1),
-        (LOWER, 1, 0, 1), (SUM, 1, 0), (SUM, 3, 0), (SUM, 1, 1), (SUM, 2, 1), (SUM, 2, 0),
+        (UPPER, 1, 0, 1), (LOWER, 0, 1, 1), (UPPER, 3, 0, 1), (LOWER, 0, 0, 1), (SUM, 0, 0), (LOWER, 1, 1, 0),
+        (SUM, 0, 1), (UPPER, 2, 0, 0), (LOWER, 3, 1, 0), (LOWER, 1, 0, 0), (LOWER, 3, 0, 0), (UPPER, 2, 0, 1),
+        (LOWER, 1, 1, 1), (LOWER, 3, 1, 1), (SUM, 1, 1), (LOWER, 1, 0, 1), (LOWER, 3, 0, 1), (SUM, 3, 1),
+        (SUM, 1, 0), (SUM, 3, 0), (SUM, 2, 0), (SUM, 2, 1),
     ),
     (
-        (LOWER, 3, 0, 0), (UPPER, 0, 0, 0), (UPPER, 0, 1, 1), (LOWER, 1, 0, 1), (LOWER, 0, 1, 0), (LOWER, 0, 1, 1),
-        (SUM, 0, 1), (UPPER, 1, 0, 0), (LOWER, 3, 1, 0), (UPPER, 1, 1, 1), (UPPER, 3, 0, 0), (LOWER, 1, 1, 1),
-        (SUM, 1, 1), (SUM, 1, 0), (UPPER, 3, 1, 1), (SUM, 3, 0), (SUM, 3, 1), (UPPER, 2, 0, 0), (UPPER, 2, 1, 1),
-        (SUM, 0, 0), (SUM, 2, 0), (SUM, 2, 1),
+        (LOWER, 1, 0, 0), (LOWER, 3, 0, 0), (UPPER, 0, 0, 0), (UPPER, 0, 1, 1), (LOWER, 1, 0, 1), (LOWER, 3, 0, 1),
+        (LOWER, 0, 1, 0), (LOWER, 0, 1, 1), (UPPER, 1, 0, 0), (SUM, 0, 1), (LOWER, 3, 1, 0), (LOWER, 1, 1, 0),
+        (UPPER, 1, 1, 1), (UPPER, 3, 0, 0), (LOWER, 3, 1, 1), (LOWER, 1, 1, 1), (SUM, 1, 1), (SUM, 1, 0),
+        (UPPER, 3, 1, 1), (SUM, 3, 0), (UPPER, 2, 0, 0), (SUM, 3, 1), (UPPER, 2, 1, 1), (SUM, 0, 0), (SUM, 2, 0),
+        (SUM, 2, 1),
     ),
     (
         (RELAY, 1), (RELAY, 0), (UPPER, 1, 0, 0), (UPPER, 3, 0, 0), (LOWER, 0, 0, 0), (LOWER, 0, 1, 0),
-        (UPPER, 1, 0, 1), (UPPER, 3, 0, 1), (LOWER, 0, 0, 1), (SUM, 0, 0), (LOWER, 0, 1, 1), (UPPER, 0, 1, 1),
-        (UPPER, 0, 1, 0), (SUM, 0, 1), (UPPER, 2, 0, 0), (LOWER, 3, 0, 0), (LOWER, 1, 0, 1), (SUM, 1, 0),
-        (LOWER, 3, 1, 0), (UPPER, 2, 0, 1), (LOWER, 1, 1, 1), (SUM, 3, 0), (SUM, 1, 1), (SUM, 3, 1), (SUM, 2, 0),
-        (SUM, 2, 1),
+        (UPPER, 1, 0, 1), (UPPER, 3, 0, 1), (LOWER, 0, 0, 1), (LOWER, 0, 1, 1), (SUM, 0, 0), (UPPER, 0, 1, 1),
+        (UPPER, 0, 1, 0), (LOWER, 1, 0, 0), (SUM, 0, 1), (UPPER, 2, 0, 0), (LOWER, 1, 1, 0), (LOWER, 3, 0, 0),
+        (LOWER, 1, 0, 1), (LOWER, 3, 1, 0), (SUM, 1, 0), (UPPER, 2, 0, 1), (LOWER, 1, 1, 1), (LOWER, 3, 0, 1),
+        (SUM, 1, 1), (SUM, 3, 0), (LOWER, 3, 1, 1), (SUM, 3, 1), (SUM, 2, 0), (SUM, 2, 1),
     ),
     (
-        (UPPER, 0, 0, 0), (UPPER, 0, 1, 1), (LOWER, 3, 0, 0), (SUM, 0, 0), (LOWER, 1, 0, 1), (LOWER, 0, 1, 1),
-        (LOWER, 0, 1, 0), (UPPER, 1, 1, 1), (UPPER, 1, 0, 0), (UPPER, 3, 0, 0), (UPPER, 3, 1, 1), (SUM, 1, 0),
-        (LOWER, 3, 1, 0), (SUM, 3, 0), (UPPER, 2, 0, 0), (LOWER, 1, 1, 1), (SUM, 1, 1), (SUM, 3, 1),
-        (UPPER, 2, 1, 1), (SUM, 0, 1), (SUM, 2, 0), (SUM, 2, 1),
+        (UPPER, 0, 0, 0), (UPPER, 0, 1, 1), (LOWER, 1, 0, 0), (LOWER, 3, 0, 0), (LOWER, 1, 0, 1), (LOWER, 3, 0, 1),
+        (LOWER, 0, 1, 1), (SUM, 0, 0), (LOWER, 0, 1, 0), (UPPER, 1, 1, 1), (UPPER, 1, 0, 0), (LOWER, 3, 1, 1),
+        (LOWER, 1, 1, 1), (UPPER, 3, 0, 0), (LOWER, 3, 1, 0), (UPPER, 3, 1, 1), (LOWER, 1, 1, 0), (SUM, 1, 1),
+        (SUM, 1, 0), (SUM, 3, 1), (UPPER, 2, 0, 0), (UPPER, 2, 1, 1), (SUM, 3, 0), (SUM, 0, 1), (SUM, 2, 0),
+        (SUM, 2, 1),
     ),
 )
 
@@ -48,8 +51,8 @@
 
 
 def kernel(
-    rows, width, re_ref, im_ref, chan_ref, count_ref, level_ref, allowed_ref, recoup_ref, out_ref,
-    up, low, transit, swapped, acc, other, coded, got, gain, got_gain, weight, mine, theirs, labels,
+    rows, width, re_ref, im_ref, chan_ref, count_ref, level_ref, allowed_ref, recoup_ref, got, got_unit,
+    up, low, transit, swapped, acc, other, coded, unit, weight, zeros, mine, theirs, labels,
     send_up, recv_up, send_low, recv_low, recv_transit, send_sum, recv_sum, send_out, recv_out, local_sem,
 ):
     live, upper, main, extra, lower = plan(rows, width)
@@ -123,7 +126,7 @@
 
         send(at_y, make)
 
-    def send_low_piece(at_y, src, part, dx, dhalf, to, count, passing=False):
+    def send_low_piece(at_y, src, part, dx, dhalf, to, count, when=None, passing=False):
         n = used["low"]
         used["low"] += 1
 
@@ -133,7 +136,8 @@
                 dst, recv = transit.at[pl.ds(part * rows, rows), pl.ds(0, count)], recv_transit.at[part]
             else:
                 dst, recv = piece(low, slab, part, count), recv_low.at[slab, part]
-            return [(slab < 7, remote(src(slab), dst, send_low.at[n], recv, device(*to)))]
+            ok = (slab < 7) if when is None else (slab < 7) & when()
+            return [(ok, remote(src(slab), dst, send_low.at[n], recv, device(*to)))]
 
         send(at_y, make)
 
@@ -172,12 +176,12 @@
     for when, copy in own:
         pl.when(when)(copy.start)
 
-    out_ref[0, :, live:] = jnp.zeros((rows, width - live), jnp.float32)
-
-    @pl.when(my_slab == 7)
-    def _():
-        out_ref[0, :, :live] = jnp.zeros((rows, live), jnp.float32)
-
+    zeros[...] = jnp.zeros_like(zeros)
+    blank = []
+    for when, columns in ((my_slab < 7, pl.ds(live, width - live)), (my_slab == 7, pl.ds(0, width))):
+        blank.append((when, pltpu.make_async_copy(zeros.at[:, columns], got_unit.at[:, columns], local_sem.at[4])))
+    for when, copy in blank:
+        pl.when(when)(copy.start)
     acc[...] = jnp.zeros_like(acc)
 
     meta_copy.wait()
@@ -246,10 +250,17 @@
 
     def go_on(at_y, kind, dx, dhalf, part):
         if kind == LOWER:
+            usual = part == (0 if dx == 3 else 1)
+            if dx == 0:
+                when = None
+            elif usual:
+                when = None if dhalf == 0 else (lambda: x != 1)
+            else:
+                when = (lambda: x == 3) if dhalf == 1 else (lambda: x < 0)
             count = low_count(at_y)
             for to_dx in ((1, 3) if dx == 0 else (4 - dx,)):
                 send_low_piece(
-                    at_y, lambda slab: piece(low, slab, part, count), part, dx, dhalf, (to_dx, 0), count)
+                    at_y, lambda slab: piece(low, slab, part, count), part, dx, dhalf, (to_dx, 0), count, when)
             return
         when = None
         if at_y % 2 == 1:
@@ -327,54 +338,48 @@
     def out_counts(of_y):
         return ((of_y < 3, main), (of_y == 3, lower))
 
-    outs = []
+    outs, kept = [], []
     for n, dy in enumerate(order):
         to_y = (y + dy) % 4
         when, copy = sums[n]
 
         @pl.when(when)
-        def _(n=n, dy=dy, to_y=to_y, copy=copy):
+        def _(n=n, to_y=to_y, copy=copy):
             copy.wait_recv()
             keep = rows_of(to_y, core)
             value = weight[keep] * (acc[to_y % 2, keep] + other[n])
-            if dy == 0:
-                for size_when, count in out_counts(y):
-                    @pl.when(size_when)
-                    def _(count=count):
-                        out_ref[0, :, pl.ds(d_start, count)] = value[:, :count]
-            else:
-                largest = jnp.max(jnp.abs(value), axis=0, keepdims=True)
-                unit = jnp.where(largest > 0.0, 1.0 / largest, 0.0)
-                coded[n] = jnp.round(value * unit * 32767.0).astype(jnp.int32).astype(jnp.int16)
-                gain[n] = largest
-
-        if dy != 0:
-            copies = [(when, remote(gain.at[n], got_gain.at[y], send_out.at[1, n], recv_out.at[1, y], device(0, dy)))]
-            for size_when, count in out_counts(y):
-                copies.append((when & size_when, remote(
-                    coded.at[n, :, pl.ds(0, count)], got.at[:, pl.ds(d_start, count)],
-                    send_out.at[0, n], recv_out.at[0, y], device(0, dy))))
-            for start_when, out in copies:
-                pl.when(start_when)(out.start)
-            outs += copies
+            largest = jnp.max(jnp.abs(value), axis=0, keepdims=True)
+            over = jnp.where(largest > 0.0, 1.0 / largest, 0.0)
+            coded[n] = jnp.round(value * over * 32767.0).astype(jnp.int32).astype(jnp.int16)
+            unit[n] = largest
+
+        for size_when, count in out_counts(y):
+            here = when & size_when
+            columns = pl.ds(d_start, count)
+            pairs = (
+                (unit.at[n, :, pl.ds(0, count)], got_unit.at[:, columns], 1),
+                (coded.at[n, :, pl.ds(0, count)], got.at[:, columns], 0),
+            )
+            for src, dst, m in pairs:
+                if dy == 0:
+                    kept.append((here, pltpu.make_async_copy(src, dst, local_sem.at[5 + m])))
+                    pl.when(here)(kept[-1][1].start)
+                else:
+                    outs.append((here, remote(src, dst, send_out.at[m, n], recv_out.at[m, y], device(0, dy))))
+                    pl.when(here)(outs[-1][1].start)
 
     have_out = (x < 3) | (half == 0)
     for dy in (1, 3, 2):
         from_y = (y + dy) % 4
-
-        @pl.when(have_out)
-        def _(from_y=from_y):
-            remote(got_gain.at[from_y], got_gain.at[from_y], send_out.at[1, 0], recv_out.at[1, from_y], device(1, 0)).wait_recv()
-
         for size_when, count in out_counts(from_y):
             @pl.when(have_out & size_when)
             def _(from_y=from_y, count=count):
                 columns = pl.ds(pl.multiple_of(from_y * main, LANES), count)
-                here = got.at[:, columns]
-                remote(here, here, send_out.at[0, 0], recv_out.at[0, from_y], device(1, 0)).wait_recv()
-                value = got[:, columns].astype(jnp.int32).astype(jnp.float32) * (1.0 / 32767.0)
-                out_ref[0, :, columns] = value * got_gain[from_y][:, :count]
-
+                for m, here in ((1, got_unit.at[:, columns]), (0, got.at[:, columns])):
+                    remote(here, here, send_out.at[m, 0], recv_out.at[m, from_y], device(1, 0)).wait_recv()
+
+    for when, copy in blank + kept:
+        pl.when(when)(copy.wait)
     for at_y in range(4):
         @pl.when(y == at_y)
         def _(at_y=at_y):
@@ -388,14 +393,14 @@
 def per_device(s_real, s_imag, chan_l, counts, jlevel, allowed, recoup):
     rows, width = s_real.shape[1:]
     live, upper, main, extra, lower = plan(rows, width)
-    vmem = pl.BlockSpec(memory_space=pltpu.VMEM)
+    vmem, anywhere = pl.BlockSpec(memory_space=pltpu.VMEM), pl.BlockSpec(memory_space=pl.ANY)
     dma = pltpu.SemaphoreType.DMA
-    return pl.pallas_call(
+    got, unit = pl.pallas_call(
         functools.partial(kernel, rows, width),
         grid=(1,),
-        out_shape=jax.ShapeDtypeStruct((1, rows, width), jnp.float32),
-        in_specs=[pl.BlockSpec(memory_space=pltpu.HBM)] * 2 + [vmem] * 5,
-        out_specs=vmem,
+        out_shape=(jax.ShapeDtypeStruct((rows, width), jnp.int16), jax.ShapeDtypeStruct((1, width), jnp.float32)),
+        in_specs=[anywhere] * 2 + [vmem] * 5,
+        out_specs=(anywhere, anywhere),
         scratch_shapes=[
             pltpu.VMEM((14 * rows, upper), jnp.bfloat16),
             pltpu.VMEM((14 * rows, lower), jnp.bfloat16),
@@ -404,10 +409,9 @@
             pltpu.VMEM((2, upper, lower), jnp.float32),
             pltpu.VMEM((4, rows, lower), jnp.float32),
             pltpu.VMEM((4, rows, lower), jnp.int16),
-            pltpu.VMEM((rows, live), jnp.int16),
-            pltpu.VMEM((4, 1, lower), jnp.float32),
             pltpu.VMEM((4, 1, lower), jnp.float32),
             pltpu.VMEM((upper, lower), jnp.float32),
+            pltpu.VMEM((1, width), jnp.float32),
             pltpu.VMEM((1, width + 2 * LANES), jnp.int32),
             pltpu.VMEM((1, width + 2 * LANES), jnp.int32),
             pltpu.VMEM((8, width + 2 * LANES), jnp.int32),
@@ -419,6 +423,8 @@
         cost_estimate=pl.CostEstimate(
             flops=16 * 7 * rows * upper * lower, bytes_accessed=8 * rows * width, transcendentals=0),
     )(s_real, s_imag, chan_l, counts[:, None], jlevel[:, None], allowed, recoup)
+    share = jnp.maximum(got.astype(jnp.float32) * (1.0 / 32767.0), -1.0)
+    return (share * unit)[None]
 
 
 def solution(mesh):

time: 88.3 us -> 86.9 us (0.984)
  local copies, waits for them, and re-layouts: 3.3 us -> 0 us
  other arithmetic: 0 us -> 3.25 us
  Pallas kernels: 83.5 us -> 82.1 us
    unnamed x1 -> x0, local copies, waits for them, and re-layouts: 3.3 us -> none
    broadcast_in_dim x0 -> x1, other arithmetic: none -> 3.25 us  [per_device(): return (share * unit)[None]]
    pallas_call x1, Pallas kernels: 83.5 us -> 82.1 us  [per_device(): pl.pallas_call(functools.partial(kernel, rows, width), grid=(1,), out_sha...]
where the time goes in v4:
time: 86.9 us; the launch traced here: 86.6 us
  Pallas kernels  82.1 us (94%)
  other arithmetic  3.25 us (4%)
  between operations  1.3 us (1%)
    pallas_call x1, Pallas kernels, per_device(): pl.pallas_call(functools.partial(kernel, rows, width), grid=(1,), out_sha...  82.1 us
    broadcast_in_dim x1, other arithmetic, per_device(): return (share * unit)[None]  3.25 us

profile of v4, /device:TPU:1, one launch (start us, length us, event | category | flops | bytes accessed | tf_op | source)
XLA Modules:
  0.0 86.6 jit_solution(6753338359008991589)
XLA Ops:
  1.3 82.1 %shard_map.73 = (s16[192,3072]{1,0:T(8,128)(2,1)}, f32[1,3072]{1,0:T(1,128)}) custom-call(bf16[1,192,3072]{2,1,0:T(8,128)(2,1)} %re_ref.1, bf16[1,192,3072]{2,1,0:T(8,128)(2,1)} %im_ref.1, s32[1,3072]{1,0:T(1,128)} %chan_ref.1, s32[1,1]{1,0:T(1,128)} %bitcast.5.count_ref, s32[1,1]{1,0:T(1,128)} %bitcast.6.level_ref, s32[32,32]{1,0:T(8,128)} %allowed_ref.1, ...), custom_call_target="tpu_custom_call" | custom-call | flops 12683575296 | bytes 4718592 | tf_op jit(solution)/shard_map/pallas_call | solution.py:398
  83.4 3.2 %multiply_bitcast_fusion = f32[1,192,3072]{2,1,0:T(8,128)} fusion(s16[192,3072]{1,0:T(8,128)(2,1)} %get-tuple-element.7, f32[3072]{0:T(1024)} %bitcast.7), kind=kLoop, calls=%fused_computation | loop fusion | flops 2359296 | bytes 3551232 | tf_op jit(solution)/shard_map/broadcast_in_dim | solution.py:427

commit v5 on v4

--- a/solution.py
+++ b/solution.py
@@ -52,6 +52,7 @@
 
 def kernel(
     rows, width, re_ref, im_ref, chan_ref, count_ref, level_ref, allowed_ref, recoup_ref, got, got_unit,
+    chan, allowed, recoup,
     up, low, transit, swapped, acc, other, coded, unit, weight, zeros, mine, theirs, labels,
     send_up, recv_up, send_low, recv_low, recv_transit, send_sum, recv_sum, send_out, recv_out, local_sem,
 ):
@@ -72,6 +73,11 @@
             src_ref=src, dst_ref=dst, send_sem=send, recv_sem=recv, device_id=where, device_id_type=MESH
         )
 
+    small = [
+        pltpu.make_async_copy(src, dst, local_sem.at[8 + n])
+        for n, (src, dst) in enumerate(((chan_ref, chan), (allowed_ref, allowed), (recoup_ref, recoup)))]
+    for copy in small:
+        copy.start()
     barrier = pltpu.get_barrier_semaphore()
     greeted = [(1, 0, 0), (3, 0, 0), (2, 0, 0), (0, 1, 0), (0, 3, 0), (0, 2, 0), (0, 0, 1)]
     for offset in greeted:
@@ -88,7 +94,9 @@
     have_rows = my_slab < 7
     up_from, low_from = is_upper & have_rows, is_lower & have_rows
 
-    mine[:, :width] = chan_ref[...]
+    for copy in small:
+        copy.wait()
+    mine[:, :width] = chan[...]
     mine[:, width:width + LANES] = jnp.broadcast_to(count_ref[...], (1, LANES))
     mine[:, width + LANES:] = jnp.broadcast_to(level_ref[...], (1, LANES))
     meta_copy = remote(mine, theirs, local_sem.at[0], local_sem.at[1], device(0, 1 - 2 * parity))
@@ -184,37 +192,11 @@
         pl.when(when)(copy.start)
     acc[...] = jnp.zeros_like(acc)
 
-    meta_copy.wait()
-    first = jnp.where(is_upper, mine[...], theirs[...])
-    second = jnp.where(is_upper, theirs[...], mine[...])
-    upper_count, lower_count = first[:, width:width + 1], second[:, width:width + 1]
-    upper_deg = (2 * first[:, width + LANES:width + LANES + 1] + 1).astype(jnp.float32)
-    lower_deg = (2 * second[:, width + LANES:width + LANES + 1] + 1).astype(jnp.float32)
-    factor = 2.0 * lower_deg / (upper_deg + lower_deg)
-    labels[0:1, :] = first
-    labels[1:2, :] = second
-    table = recoup_ref[...] * allowed_ref[...].astype(jnp.float32)
-    levels = table.shape[0]
-    c_start = pl.multiple_of(x * upper, LANES)
-    d_start = pl.multiple_of(y * main, LANES)
-    c_labels = labels[0:1, pl.ds(c_start, upper)]
-    d_labels = labels[1:2, pl.ds(d_start, lower)]
-    c_open = c_start + lax.broadcasted_iota(jnp.int32, (1, upper), 1) < upper_count
-    d_open = d_start + lax.broadcasted_iota(jnp.int32, (1, lower), 1) < lower_count
-    c_labels = jnp.where(c_open, c_labels, -1)
-    d_labels = jnp.where(d_open, d_labels, -1)
-    c_hot = (lax.broadcasted_iota(jnp.int32, (levels, upper), 0) == c_labels).astype(jnp.float32)
-    d_hot = (lax.broadcasted_iota(jnp.int32, (levels, lower), 0) == d_labels).astype(jnp.float32)
-    picked = factor * jnp.dot(
-        table, d_hot, precision=lax.Precision.HIGHEST, preferred_element_type=jnp.float32)
-    weight[...] = lax.dot_general(
-        c_hot, picked, (((0,), (0,)), ((), ())),
-        precision=lax.Precision.HIGHEST, preferred_element_type=jnp.float32)
-    least = jnp.minimum(upper_count, lower_count)
     for when, copy in own:
         pl.when(when)(copy.wait)
 
     tile = min(256, upper)
+    limits = []
 
     def accumulate(slab):
         @pl.when(slab < 7)
@@ -222,7 +204,7 @@
             row = pl.multiple_of(slab * 2 * rows, rows)
             first_row = (slab // 2) * (4 * rows) + (slab % 2) * (2 * rows) + core * rows
             row_ids = first_row + lax.broadcasted_iota(jnp.int32, (rows, lower), 0)
-            keep = (row_ids < least).astype(jnp.float32).astype(jnp.bfloat16)
+            keep = (row_ids < limits[0]).astype(jnp.float32).astype(jnp.bfloat16)
             low_re = low[pl.ds(row, rows)] * keep
             low_im = low[pl.ds(pl.multiple_of(row + rows, rows), rows)] * keep
             swapped[0, :rows] = low_re
@@ -319,6 +301,35 @@
             events = steps(at_y)[n]
             pl.when(y == at_y)(functools.partial(react, at_y, events))
             slab = jnp.where(y == at_y, slab_at(*events[-1][1:]), slab)
+        if n == 0:
+            meta_copy.wait()
+            first = jnp.where(is_upper, mine[...], theirs[...])
+            second = jnp.where(is_upper, theirs[...], mine[...])
+            upper_count, lower_count = first[:, width:width + 1], second[:, width:width + 1]
+            upper_deg = (2 * first[:, width + LANES:width + LANES + 1] + 1).astype(jnp.float32)
+            lower_deg = (2 * second[:, width + LANES:width + LANES + 1] + 1).astype(jnp.float32)
+            factor = 2.0 * lower_deg / (upper_deg + lower_deg)
+            labels[0:1, :] = first
+            labels[1:2, :] = second
+            table = recoup[...] * allowed[...].astype(jnp.float32)
+            levels = table.shape[0]
+            c_start = pl.multiple_of(x * upper, LANES)
+            d_start = pl.multiple_of(y * main, LANES)
+            c_labels = labels[0:1, pl.ds(c_start, upper)]
+            d_labels = labels[1:2, pl.ds(d_start, lower)]
+            c_open = c_start + lax.broadcasted_iota(jnp.int32, (1, upper), 1) < upper_count
+            d_open = d_start + lax.broadcasted_iota(jnp.int32, (1, lower), 1) < lower_count
+            c_labels = jnp.where(c_open, c_labels, -1)
+            d_labels = jnp.where(d_open, d_labels, -1)
+            c_hot = (lax.broadcasted_iota(jnp.int32, (levels, upper), 0) == c_labels).astype(jnp.float32)
+            d_hot = (lax.broadcasted_iota(jnp.int32, (levels, lower), 0) == d_labels).astype(jnp.float32)
+            picked = factor * jnp.dot(
+                table, d_hot, precision=lax.Precision.HIGHEST, preferred_element_type=jnp.float32)
+            weight[...] = lax.dot_general(
+                c_hot, picked, (((0,), (0,)), ((), ())),
+                precision=lax.Precision.HIGHEST, preferred_element_type=jnp.float32)
+            least = jnp.minimum(upper_count, lower_count)
+            limits.append(least)
         accumulate(slab)
 
     order = (2, 1, 3, 0)
@@ -399,9 +410,12 @@
         functools.partial(kernel, rows, width),
         grid=(1,),
         out_shape=(jax.ShapeDtypeStruct((rows, width), jnp.int16), jax.ShapeDtypeStruct((1, width), jnp.float32)),
-        in_specs=[anywhere] * 2 + [vmem] * 5,
+        in_specs=[anywhere] * 3 + [vmem] * 2 + [anywhere] * 2,
         out_specs=(anywhere, anywhere),
         scratch_shapes=[
+            pltpu.VMEM(chan_l.shape, jnp.int32),
+            pltpu.VMEM(allowed.shape, jnp.int32),
+            pltpu.VMEM(recoup.shape, jnp.float32),
             pltpu.VMEM((14 * rows, upper), jnp.bfloat16),
             pltpu.VMEM((14 * rows, lower), jnp.bfloat16),
             pltpu.VMEM((2 * rows, lower), jnp.bfloat16),
@@ -416,7 +430,7 @@
             pltpu.VMEM((1, width + 2 * LANES), jnp.int32),
             pltpu.VMEM((8, width + 2 * LANES), jnp.int32),
             dma((40,)), dma((7, 2)), dma((40,)), dma((7, 2)), dma((2,)),
-            dma((4,)), dma((4,)), dma((2, 4)), dma((2, 4)), dma((8,)),
+            dma((4,)), dma((4,)), dma((2, 4)), dma((2, 4)), dma((12,)),
         ],
         compiler_params=pltpu.CompilerParams(
             collective_id=0, has_side_effects=True, vmem_limit_bytes=61 << 20),

time: 86.9 us -> 86.3 us (level)
  no operation moved by 1% of the time
where the time goes in v5:
time: 86.3 us; the launch traced here: 86.1 us
  Pallas kernels  81.6 us (95%)
  other arithmetic  3.25 us (4%)
  between operations  1.3 us (2%)
    pallas_call x1, Pallas kernels, per_device(): pl.pallas_call(functools.partial(kernel, rows, width), grid=(1,), out_sha...  81.6 us
    broadcast_in_dim x1, other arithmetic, per_device(): return (share * unit)[None]  3.25 us

profile of v5, /device:TPU:1, one launch (start us, length us, event | category | flops | bytes accessed | tf_op | source)
XLA Modules:
  0.0 86.1 jit_solution(5839645541229216715)
XLA Ops:
  1.3 81.6 %shard_map.73 = (s16[192,3072]{1,0:T(8,128)(2,1)}, f32[1,3072]{1,0:T(1,128)}) custom-call(bf16[1,192,3072]{2,1,0:T(8,128)(2,1)} %re_ref.1, bf16[1,192,3072]{2,1,0:T(8,128)(2,1)} %im_ref.1, s32[1,3072]{1,0:T(1,128)} %chan_ref.1, s32[1,1]{1,0:T(1,128)} %bitcast.5.count_ref, s32[1,1]{1,0:T(1,128)} %bitcast.6.level_ref, s32[32,32]{1,0:T(8,128)} %allowed_ref.1, ...), custom_call_target="tpu_custom_call" | custom-call | flops 12683575296 | bytes 4718592 | tf_op jit(solution)/shard_map/pallas_call | solution.py:409
  82.9 3.2 %multiply_bitcast_fusion = f32[1,192,3072]{2,1,0:T(8,128)} fusion(s16[192,3072]{1,0:T(8,128)(2,1)} %get-tuple-element.7, f32[3072]{0:T(1024)} %bitcast.7), kind=kLoop, calls=%fused_computation | loop fusion | flops 2359296 | bytes 3551232 | tf_op jit(solution)/shard_map/broadcast_in_dim | solution.py:441

commit v6 on v5

--- a/solution.py
+++ b/solution.py
@@ -332,7 +332,7 @@
             limits.append(least)
         accumulate(slab)
 
-    order = (2, 1, 3, 0)
+    order = (2, 3 - 2 * parity, 1 + 2 * parity, 0)
 
     def rows_of(to_y, of_core):
         return pl.ds(pl.multiple_of((to_y // 2) * (2 * rows) + of_core * rows, rows), rows)
@@ -372,7 +372,7 @@
                 (coded.at[n, :, pl.ds(0, count)], got.at[:, columns], 0),
             )
             for src, dst, m in pairs:
-                if dy == 0:
+                if n == 3:
                     kept.append((here, pltpu.make_async_copy(src, dst, local_sem.at[5 + m])))
                     pl.when(here)(kept[-1][1].start)
                 else:

time: 86.3 us -> 86.3 us (level)
  no operation moved by 1% of the time
where the time goes in v6:
time: 86.3 us; the launch traced here: 86.2 us
  Pallas kernels  81.6 us (95%)
  other arithmetic  3.25 us (4%)
  between operations  1.3 us (2%)
    pallas_call x1, Pallas kernels, per_device(): pl.pallas_call(functools.partial(kernel, rows, width), grid=(1,), out_sha...  81.6 us
    broadcast_in_dim x1, other arithmetic, per_device(): return (share * unit)[None]  3.25 us

profile of v6, /device:TPU:1, one launch (start us, length us, event | category | flops | bytes accessed | tf_op | source)
XLA Modules:
  0.0 86.2 jit_solution(1301603536671899270)
XLA Ops:
  1.3 81.6 %shard_map.73 = (s16[192,3072]{1,0:T(8,128)(2,1)}, f32[1,3072]{1,0:T(1,128)}) custom-call(bf16[1,192,3072]{2,1,0:T(8,128)(2,1)} %re_ref.1, bf16[1,192,3072]{2,1,0:T(8,128)(2,1)} %im_ref.1, s32[1,3072]{1,0:T(1,128)} %chan_ref.1, s32[1,1]{1,0:T(1,128)} %bitcast.5.count_ref, s32[1,1]{1,0:T(1,128)} %bitcast.6.level_ref, s32[32,32]{1,0:T(8,128)} %allowed_ref.1, ...), custom_call_target="tpu_custom_call" | custom-call | flops 12683575296 | bytes 4718592 | tf_op jit(solution)/shard_map/pallas_call | solution.py:409
  82.9 3.2 %multiply_bitcast_fusion = f32[1,192,3072]{2,1,0:T(8,128)} fusion(s16[192,3072]{1,0:T(8,128)(2,1)} %get-tuple-element.7, f32[3072]{0:T(1024)} %bitcast.7), kind=kLoop, calls=%fused_computation | loop fusion | flops 2359296 | bytes 3551232 | tf_op jit(solution)/shard_map/broadcast_in_dim | solution.py:441
